TPU v7x, 256 devices: a whole 4x4x8 slice. The times are simulated.
256 devices in a mesh: seq: 64 (over z, x, core), ffn: 4 (over y).
Axes of the slice: x: 4, y: 4, z: 8, core: 2. Of those that a mesh axis runs over, the one named last changes fastest.
Arguments:
- tokens: bfloat16 [64, 256, 8192], P('seq', None, 'ffn'), may hold values from -6 to 6
- cotangent: bfloat16 [64, 256, 8192], P('seq', None, 'ffn'), may hold values from -6 to 6
- block_masks: int32 [64, 128], replicated, may hold values from 0 to 1, as said below
- w_up: bfloat16 [8192, 16384], P('ffn', 'seq'), may hold values from -0.0625 to 0.0625
- w_gate: bfloat16 [8192, 16384], P('ffn', 'seq'), may hold values from -0.0625 to 0.0625
- w_down: bfloat16 [16384, 8192], P('seq', 'ffn'), may hold values from -0.25 to 0.25
Outputs:
- outputs: bfloat16 [64, 256, 8192], P('seq', None, 'ffn')
- grad_tokens: bfloat16 [64, 256, 8192], P('seq', None, 'ffn')
- grad_up: bfloat16 [8192, 16384], P('ffn', 'seq')
- grad_gate: bfloat16 [8192, 16384], P('ffn', 'seq')
- grad_down: bfloat16 [16384, 8192], P('seq', 'ffn')
Inputs may be any that keep to these rules, and one draw needn't show every extreme that they name: `block_masks`: split the 128 blocks into runs of 2 consecutive blocks (owners). For every owner, between 1 and 3 groups have any block of that owner active, and some owner has exactly 3.
All inputs are finite; a program needn't handle non-finite values.
Results may differ from a plain program's by a relative error of at most 0.005.
Values may be sent and summed in bfloat16 or wider, within the bound.
A program may use at most 128 MiB of HBM per device.

v0:
```python
import jax
import jax.numpy as jnp
from jax import lax
from jax.sharding import PartitionSpec as P

BLK = 128
CAP = 3


def contract_rows(left_side, right_side):
    return lax.dot_general(
        left_side, right_side, (((0,), (0,)), ((), ())), preferred_element_type=jnp.float32
    )


def contract_cols(left_side, right_side):
    return lax.dot_general(
        left_side, right_side, (((1,), (1,)), ((), ())), preferred_element_type=jnp.float32
    )


def settle(returned, select_map):
    summed = jnp.einsum("sg,spw->gpw", select_map, returned, precision=lax.Precision.HIGHEST)
    return summed.astype(jnp.bfloat16)


def body(tokens, cotangent, block_masks, w_up, w_gate, w_down):
    owners = lax.axis_size("seq")
    grp_dev, group_len, slice_width = tokens.shape
    groups = block_masks.shape[0]
    unit_count = w_up.shape[1]
    owner_blocks = unit_count // BLK
    row_count = CAP * group_len
    my_owner = lax.axis_index("seq")
    spread_tokens, spread_cotan = (
        lax.all_to_all(tokens, "seq", split_axis=1, concat_axis=0, tiled=True),
        lax.all_to_all(cotangent, "seq", split_axis=1, concat_axis=0, tiled=True),
    )
    active = jnp.max(block_masks.reshape(groups, owners, owner_blocks), axis=2).T
    ordinal = jnp.cumsum(active, axis=1) - 1
    slot_ids = jnp.arange(CAP, dtype=jnp.int32)
    picked = ((ordinal[:, None, :] == slot_ids[None, :, None]) & (active[:, None, :] > 0)).astype(
        jnp.int32
    )
    group_ids = jnp.arange(groups, dtype=jnp.int32)
    slot_group = jnp.sum(picked * group_ids[None, None, :], axis=2)
    lookup = slot_group.T
    packed_tokens = spread_tokens[lookup]
    packed_cotan = spread_cotan[lookup]
    token_rows, cotan_rows = (
        lax.all_to_all(packed_tokens, "seq", split_axis=1, concat_axis=1, tiled=True),
        lax.all_to_all(packed_cotan, "seq", split_axis=1, concat_axis=1, tiled=True),
    )
    token_rows = token_rows.reshape(row_count, slice_width)
    cotan_rows = cotan_rows.reshape(row_count, slice_width)
    my_picked = lax.dynamic_index_in_dim(picked, my_owner, 0, keepdims=False).astype(jnp.float32)
    my_columns = lax.dynamic_slice_in_dim(
        block_masks, my_owner * owner_blocks, owner_blocks, 1
    ).astype(jnp.float32)
    block_live = jnp.dot(my_picked, my_columns, preferred_element_type=jnp.float32)
    unit_live = jnp.repeat(block_live, BLK, axis=1)
    row_mask = jnp.broadcast_to(unit_live[:, None, :], (CAP, group_len, unit_count)).reshape(
        row_count, unit_count
    )
    up_part = jnp.dot(token_rows, w_up, preferred_element_type=jnp.float32)
    gate_part = jnp.dot(token_rows, w_gate, preferred_element_type=jnp.float32)
    up_full, gate_full = lax.psum((up_part, gate_part), "ffn")
    rectified = jnp.maximum(gate_full, 0.0)
    hidden = (rectified * rectified * up_full * row_mask).astype(jnp.bfloat16)
    out_part = jnp.dot(hidden, w_down, preferred_element_type=jnp.float32).reshape(
        CAP, group_len, slice_width
    )
    select_map = picked.reshape(owners * CAP, groups).astype(jnp.float32)
    hidden_part = contract_cols(cotan_rows, w_down)
    hidden_grad = lax.psum(hidden_part, "ffn") * row_mask
    up_grad = (hidden_grad * rectified * rectified).astype(jnp.bfloat16)
    gate_grad = (hidden_grad * up_full * 2.0 * rectified).astype(jnp.bfloat16)
    input_part = contract_cols(up_grad, w_up) + contract_cols(gate_grad, w_gate)
    input_part = input_part.reshape(CAP, group_len, slice_width)
    grad_scale = 1.0 / group_len
    grad_up = (contract_rows(token_rows, up_grad) * grad_scale).astype(jnp.bfloat16)
    grad_gate = (contract_rows(token_rows, gate_grad) * grad_scale).astype(jnp.bfloat16)
    grad_down = (contract_rows(hidden, cotan_rows) * grad_scale).astype(jnp.bfloat16)
    out_back, input_back = (
        lax.all_to_all(out_part, "seq", split_axis=1, concat_axis=0, tiled=True),
        lax.all_to_all(input_part, "seq", split_axis=1, concat_axis=0, tiled=True),
    )
    out_settled = settle(out_back, select_map)
    grad_settled = settle(input_back, select_map)
    outputs, grad_tokens = (
        lax.all_to_all(out_settled, "seq", split_axis=0, concat_axis=1, tiled=True),
        lax.all_to_all(grad_settled, "seq", split_axis=0, concat_axis=1, tiled=True),
    )
    return (outputs, grad_tokens, grad_up, grad_gate, grad_down)


def solution(mesh):
    in_specs = (
        P("seq", None, "ffn"),
        P("seq", None, "ffn"),
        P(),
        P("ffn", "seq"),
        P("ffn", "seq"),
        P("seq", "ffn"),
    )
    out_specs = (
        P("seq", None, "ffn"),
        P("seq", None, "ffn"),
        P("ffn", "seq"),
        P("ffn", "seq"),
        P("seq", "ffn"),
    )
    return jax.shard_map(body, mesh=mesh, in_specs=in_specs, out_specs=out_specs, check_vma=False)
```

profile of v0, /device:TPU:1, one launch (start us, length us, event | category | flops | bytes accessed | tf_op | source)
XLA Modules:
  0.0 823.9 jit_solution(7049187886932168033)
XLA Ops:
  7.2 2.9 copy.93
  10.6 7.8 reduce.4
  18.4 2.6 reshape.99
  21.0 13.6 %all-to-all-start = ((bf16[64,2,4096]{2,1,0:T(2,128)(2,1)}), bf16[64,2,4096]{2,1,0:T(2,128)(2,1)}, u32[]{:S(2)}, u32[]{:S(2)}) async-start(bf16[64,2,4096]{2,1,0:T(2,128)(2,1)} %reshape.99), calls=%async_computation | async-start | bytes 2097152 | tf_op jit(solution)/shard_map/all_to_all | solution.py:36
  34.6 2.8 copy.92
  37.5 7.8 reduce.5
  45.3 2.6 reshape.101
  47.9 14.4 %all-to-all-done = bf16[64,2,4096]{2,1,0:T(2,128)(2,1)} async-done(((bf16[64,2,4096]{2,1,0:T(2,128)(2,1)}), bf16[64,2,4096]{2,1,0:T(2,128)(2,1)}, u32[]{:S(2)}, u32[]{:S(2)}) %all-to-all-start) | async-done | bytes 1048608 | tf_op jit(solution)/shard_map/all_to_all | solution.py:36
  62.3 7.3 all-to-all-start.4
  71.4 6.5 reshape.100
  77.9 7.0 bitcast_reduce_fusion.1
  85.0 1.5 all_to_all.65
  86.4 9.7 %gather_fusion = bf16[192,4,2048]{2,1,0:T(4,128)(2,1)} fusion(bf16[64,4,2048]{2,1,0:T(4,128)(2,1)S(1)} %all_to_all.65, s32[1024]{0:T(1024)S(1)} %pad_clamp_fusion), kind=kCustom, calls=%fused_computation | custom fusion | bytes 6292224 | tf_op jit(solution)/shard_map/gather | solution.py:48
  96.2 5.2 copy.41
  101.4 10.5 %all-to-all-start.1 = ((bf16[3,64,4,2048]{3,2,0,1:T(4,128)(2,1)}), bf16[3,64,4,2048]{3,2,0,1:T(4,128)(2,1)}, u32[]{:S(2)}, u32[]{:S(2)}) async-start(bf16[3,64,4,2048]{3,2,0,1:T(4,128)(2,1)} %copy.41), calls=%async_computation.1 | async-start | bytes 6291456 | tf_op jit(solution)/shard_map/all_to_all | solution.py:51
  111.8 6.5 reshape.102
  118.3 7.0 bitcast_reduce_fusion
  126.9 10.0 %gather_fusion.1 = bf16[192,4,2048]{2,1,0:T(4,128)(2,1)} fusion(bf16[64,4,2048]{2,1,0:T(4,128)(2,1)S(1)} %all_to_all.73, s32[1024]{0:T(1024)S(1)} %pad_clamp_fusion), kind=kCustom, calls=%fused_computation.1 | custom fusion | bytes 6292224 | tf_op jit(solution)/shard_map/gather | solution.py:49
  136.8 5.1 copy.51
  142.0 42.3 %all-to-all-done.1 = bf16[3,64,4,2048]{3,2,0,1:T(4,128)(2,1)} async-done(((bf16[3,64,4,2048]{3,2,0,1:T(4,128)(2,1)}), bf16[3,64,4,2048]{3,2,0,1:T(4,128)(2,1)}, u32[]{:S(2)}, u32[]{:S(2)}) %all-to-all-start.1) | async-done | bytes 3145760 | tf_op jit(solution)/shard_map/all_to_all | solution.py:51
  184.3 6.8 all-to-all-start.5
  191.2 5.5 copy.42
  196.7 5.5 reshape.68
  202.2 3.9 fusion.36
  206.1 1.9 fusion.35
  208.0 55.8 %all-to-all-done.5 = bf16[3,64,4,2048]{3,2,0,1:T(4,128)(2,1)} async-done(((bf16[3,64,4,2048]{3,2,0,1:T(4,128)(2,1)}), bf16[3,64,4,2048]{3,2,0,1:T(4,128)(2,1)}, u32[]{:S(2)}, u32[]{:S(2)}) %all-to-all-start.5) | async-done | bytes 3145760 | tf_op jit(solution)/shard_map/all_to_all | solution.py:52
  263.8 5.5 copy.52
  269.3 5.6 reshape.71
  274.8 3.8 fusion.38
  279.0 65.7 %all-reduce.3.cloned.1.call-done = (f32[768,256]{1,0:T(8,128)}, f32[768,256]{1,0:T(8,128)}, f32[768,256]{1,0:T(8,128)}) async-done(((f32[768,256]{1,0:T(8,128)}, f32[768,256]{1,0:T(8,128)}, f32[768,256]{1,0:T(8,128)}), (f32[768,256]{1,0:T(8,128)}, f32[768,256]{1,0:T(8,128)}, f32[768,256]{1,0:T(8,128)})) %all-reduce.3.cloned.1.call-update) | async-done | bytes 2359312 | tf_op jit(solution)/shard_map/psum | solution.py:67
  344.7 1.9 multiply_convert_fusion
  349.1 7.5 copy.53
  356.7 10.9 %all-to-all-start.6 = ((f32[3,256,2048]{2,0,1:T(4,128)}), f32[3,256,2048]{2,0,1:T(4,128)}, u32[]{:S(2)}, u32[]{:S(2)}) async-start(f32[3,256,2048]{2,0,1:T(4,128)} %copy.53), calls=%async_computation.6 | async-start | bytes 16777216 | tf_op jit(solution)/shard_map/all_to_all | solution.py:86
  368.5 7.6 copy.44
  376.1 173.8 %all-to-all-done.6 = f32[3,256,2048]{2,0,1:T(4,128)} async-done(((f32[3,256,2048]{2,0,1:T(4,128)}), f32[3,256,2048]{2,0,1:T(4,128)}, u32[]{:S(2)}, u32[]{:S(2)}) %all-to-all-start.6) | async-done | bytes 6291488 | tf_op jit(solution)/shard_map/all_to_all | solution.py:86
  549.9 10.6 %all-to-all-start.2 = ((f32[3,256,2048]{2,0,1:T(4,128)}), f32[3,256,2048]{2,0,1:T(4,128)}, u32[]{:S(2)}, u32[]{:S(2)}) async-start(f32[3,256,2048]{2,0,1:T(4,128)} %copy.44), calls=%async_computation.2 | async-start | bytes 16777216 | tf_op jit(solution)/shard_map/all_to_all | solution.py:85
  560.7 10.6 %fusion.15 = bf16[64,4,2048]{2,0,1:T(8,128)(2,1)S(1)} fusion(f32[3,64,4,2048]{3,0,2,1:T(4,128)} %bitcast.15, f32[64,3,64]{0,2,1:T(8,128)S(1)} %copy.47), kind=kOutput, calls=%fused_computation.17 | convolution fusion | flops 1208483840 | bytes 7389184 | tf_op jit(solution)/shard_map/sg,spw->gpw/dot_general | solution.py:23
  571.3 1.8 copy.57
  573.0 169.8 %all-to-all-done.2 = f32[3,256,2048]{2,0,1:T(4,128)} async-done(((f32[3,256,2048]{2,0,1:T(4,128)}), f32[3,256,2048]{2,0,1:T(4,128)}, u32[]{:S(2)}, u32[]{:S(2)}) %all-to-all-start.2) | async-done | bytes 6291488 | tf_op jit(solution)/shard_map/all_to_all | solution.py:85
  742.9 10.3 %all-to-all-start.7 = ((bf16[64,4,2048]{2,1,0:T(4,128)(2,1)}), bf16[64,4,2048]{2,1,0:T(4,128)(2,1)S(1)}, u32[]{:S(2)}, u32[]{:S(2)}) async-start(bf16[64,4,2048]{2,1,0:T(4,128)(2,1)} %copy.57), calls=%async_computation.7 | async-start | bytes 2097152 | tf_op jit(solution)/shard_map/all_to_all | solution.py:92
  753.2 10.6 %fusion.18 = bf16[64,4,2048]{2,0,1:T(8,128)(2,1)S(1)} fusion(f32[3,64,4,2048]{3,0,2,1:T(4,128)} %bitcast.8, f32[64,3,64]{0,2,1:T(8,128)S(1)} %copy.47), kind=kOutput, calls=%fused_computation.18 | convolution fusion | flops 1208483840 | bytes 7389184 | tf_op jit(solution)/shard_map/sg,spw->gpw/dot_general | solution.py:23
  763.8 1.8 copy.48
  765.6 15.5 %all-to-all-done.7 = bf16[64,4,2048]{2,1,0:T(4,128)(2,1)S(1)} async-done(((bf16[64,4,2048]{2,1,0:T(4,128)(2,1)}), bf16[64,4,2048]{2,1,0:T(4,128)(2,1)S(1)}, u32[]{:S(2)}, u32[]{:S(2)}) %all-to-all-start.7) | async-done | bytes 1048608 | tf_op jit(solution)/shard_map/all_to_all | solution.py:92
  781.1 6.5 all-to-all-start.3
  787.6 4.1 fusion.14
  791.7 2.1 fusion.13
  793.8 2.1 fusion.12
  796.9 18.6 %all-to-all-done.3 = bf16[64,4,2048]{2,1,0:T(4,128)(2,1)S(1)} async-done(((bf16[64,4,2048]{2,1,0:T(4,128)(2,1)}), bf16[64,4,2048]{2,1,0:T(4,128)(2,1)S(1)}, u32[]{:S(2)}, u32[]{:S(2)}) %all-to-all-start.3) | async-done | bytes 1048608 | tf_op jit(solution)/shard_map/all_to_all | solution.py:91
  (47 shorter events, 9.9 us)
Async XLA Ops:
  7.2 195.0 %copy-start = (bf16[2048,256]{1,0:T(8,128)(2,1)S(1)}, bf16[2048,256]{1,0:T(8,128)(2,1)}, u32[]{:S(2)}) copy-start(bf16[2048,256]{1,0:T(8,128)(2,1)} %param.9) | copy-start | bytes 3145732
  21.0 41.3 %all-to-all-start = ((bf16[64,2,4096]{2,1,0:T(2,128)(2,1)}), bf16[64,2,4096]{2,1,0:T(2,128)(2,1)}, u32[]{:S(2)}, u32[]{:S(2)}) async-start(bf16[64,2,4096]{2,1,0:T(2,128)(2,1)} %reshape.99), calls=%async_computation | async-start | bytes 2097152 | tf_op jit(solution)/shard_map/all_to_all | solution.py:36
  37.5 32.1 %copy-start.10 = (s32[64,128]{1,0:T(8,128)S(1)}, s32[64,128]{1,0:T(8,128)}, u32[]{:S(2)}) copy-start(s32[64,128]{1,0:T(8,128)} %param.8) | copy-start | bytes 98308
  62.3 39.0 %all-to-all-start.4 = ((bf16[64,2,4096]{2,1,0:T(2,128)(2,1)}), bf16[64,2,4096]{2,1,0:T(2,128)(2,1)}, u32[]{:S(2)}, u32[]{:S(2)}) async-start(bf16[64,2,4096]{2,1,0:T(2,128)(2,1)} %reshape.101), calls=%async_computation.4 | async-start | bytes 2097152 | tf_op jit(solution)/shard_map/all_to_all | solution.py:37
  101.4 83.0 %all-to-all-start.1 = ((bf16[3,64,4,2048]{3,2,0,1:T(4,128)(2,1)}), bf16[3,64,4,2048]{3,2,0,1:T(4,128)(2,1)}, u32[]{:S(2)}, u32[]{:S(2)}) async-start(bf16[3,64,4,2048]{3,2,0,1:T(4,128)(2,1)} %copy.41), calls=%async_computation.1 | async-start | bytes 6291456 | tf_op jit(solution)/shard_map/all_to_all | solution.py:51
  184.3 79.4 %all-to-all-start.5 = ((bf16[3,64,4,2048]{3,2,0,1:T(4,128)(2,1)}), bf16[3,64,4,2048]{3,2,0,1:T(4,128)(2,1)}, u32[]{:S(2)}, u32[]{:S(2)}) async-start(bf16[3,64,4,2048]{3,2,0,1:T(4,128)(2,1)} %copy.51), calls=%async_computation.5 | async-start | bytes 6291456 | tf_op jit(solution)/shard_map/all_to_all | solution.py:52
  191.1 153.6 %all-reduce.3.cloned.1.call-start = ((), (), s32[]{:S(2)}) async-start(), calls=%async_computation.8 | async-start | bytes 4718592 | tf_op jit(solution)/shard_map/psum | solution.py:67
  202.2 3.9 copy-start.2
  202.2 3.9 copy-start.8
  269.3 5.6 copy-start.7
  346.6 1.1 copy-start.5
  346.6 20.9 %copy-start.4 = (bf16[768,256]{1,0:T(8,128)(2,1)}, bf16[768,256]{1,0:T(8,128)(2,1)S(1)}, u32[]{:S(2)}) copy-start(bf16[768,256]{1,0:T(8,128)(2,1)S(1)} %get-tuple-element.10) | copy-start | bytes 1179652
  346.6 1.5 copy-start.9
  356.7 193.2 %all-to-all-start.6 = ((f32[3,256,2048]{2,0,1:T(4,128)}), f32[3,256,2048]{2,0,1:T(4,128)}, u32[]{:S(2)}, u32[]{:S(2)}) async-start(f32[3,256,2048]{2,0,1:T(4,128)} %copy.53), calls=%async_computation.6 | async-start | bytes 16777216 | tf_op jit(solution)/shard_map/all_to_all | solution.py:86
  549.9 193.0 %all-to-all-start.2 = ((f32[3,256,2048]{2,0,1:T(4,128)}), f32[3,256,2048]{2,0,1:T(4,128)}, u32[]{:S(2)}, u32[]{:S(2)}) async-start(f32[3,256,2048]{2,0,1:T(4,128)} %copy.44), calls=%async_computation.2 | async-start | bytes 16777216 | tf_op jit(solution)/shard_map/all_to_all | solution.py:85
  742.9 38.2 %all-to-all-start.7 = ((bf16[64,4,2048]{2,1,0:T(4,128)(2,1)}), bf16[64,4,2048]{2,1,0:T(4,128)(2,1)S(1)}, u32[]{:S(2)}, u32[]{:S(2)}) async-start(bf16[64,4,2048]{2,1,0:T(4,128)(2,1)} %copy.57), calls=%async_computation.7 | async-start | bytes 2097152 | tf_op jit(solution)/shard_map/all_to_all | solution.py:92
  765.6 26.1 %copy-start.6 = (bf16[768,256]{1,0:T(8,128)(2,1)S(1)}, bf16[768,256]{1,0:T(8,128)(2,1)}, u32[]{:S(2)}) copy-start(bf16[768,256]{1,0:T(8,128)(2,1)} %copy-done.5) | copy-start | bytes 1179652
  781.1 34.5 %all-to-all-start.3 = ((bf16[64,4,2048]{2,1,0:T(4,128)(2,1)}), bf16[64,4,2048]{2,1,0:T(4,128)(2,1)S(1)}, u32[]{:S(2)}, u32[]{:S(2)}) async-start(bf16[64,4,2048]{2,1,0:T(4,128)(2,1)} %copy.48), calls=%async_computation.3 | async-start | bytes 2097152 | tf_op jit(solution)/shard_map/all_to_all | solution.py:91
  787.6 4.1 copy-start.3
  793.8 22.9 %copy-start.1 = (bf16[2048,256]{1,0:T(8,128)(2,1)S(1)}, bf16[2048,256]{1,0:T(8,128)(2,1)}, u32[]{:S(2)}) copy-start(bf16[2048,256]{1,0:T(8,128)(2,1)} %param.9) | copy-start | bytes 3145732
Sparse Core Ops, SparseCore 0:
  278.8 65.8 all-reduce.2
where the time goes:
time: 833 us; the launch traced here: 824 us
  waiting for transfers between devices  556 us (67%)
  local copies, waits for them, and re-layouts  115 us (14%)
  starting transfers between devices  76.4 us (9%)
  matrix products  42.2 us (5%)
  other arithmetic  19 us (2%)
  between operations  14.8 us (2%)
    all_to_all x1, waiting for transfers between devices, body(): lax.all_to_all(input_part, 'seq', split_axis=1, concat_axis=0, tiled=True)  174 us
    all_to_all x1, waiting for transfers between devices, body(): lax.all_to_all(out_part, 'seq', split_axis=1, concat_axis=0, tiled=True)  170 us
    psum x1, waiting for transfers between devices, body(): up_full, gate_full = lax.psum((up_part, gate_part), 'ffn')  65.7 us
    all_to_all x1, waiting for transfers between devices, body(): lax.all_to_all(packed_cotan, 'seq', split_axis=1, concat_axis=1, tiled=True)  55.8 us
    all_to_all x1, waiting for transfers between devices, body(): lax.all_to_all(packed_tokens, 'seq', split_axis=1, concat_axis=1, tiled=T...  42.3 us
    unnamed x32, local copies, waits for them, and re-layouts  25.3 us
    dot_general x2, matrix products, settle(): jnp.einsum('sg,spw->gpw', select_map, returned, precision=lax.Precision.H...  21.2 us
    all_to_all x1, waiting for transfers between devices, body(): lax.all_to_all(out_settled, 'seq', split_axis=0, concat_axis=1, tiled=True)  18.6 us
  transfers between devices with their start and end apart: 9, of which 8 were waited for; matrix products, arithmetic and copies ran while one was open for 16% of the time, Pallas kernels for 0%

commit v1 on v0

v1 whole, which is shorter than its diff:
```python
import functools

import jax
import jax.numpy as jnp
from jax import lax
from jax.experimental import pallas as pl
from jax.experimental.pallas import tpu as pltpu
from jax.sharding import PartitionSpec as P

BLK = 128
CAP = 3
PLANE = 8
ROWS = 16
CHUNKS = 2
MESH = pl.DeviceIdType.MESH
F32, BF16 = jnp.float32, jnp.bfloat16


def dot(left, right, dims):
    return lax.dot_general(left, right, (((dims[0],), (dims[1],)), ((), ())), preferred_element_type=F32)


def kernel(Z, S, Y, W, U, slots, column_group, row_mask, tok, cot, wu_in, wg_in, wd_in,
           out, gtok, gu_out, gg_out, gd_out,
           ag0, ag1, ag2, ag3, pk0, pk1, rw0, rw1, rw2, rw3, wu, wg, wd, part, py0, py1, act0, act1,
           op0, op1, pr0, pr1, pr2, pr3, rs0, rs1, first0, first1, fin0, fin1, fin2, fin3, sel,
           w_sem, sp_send, sp_recv, ag_send, ag_recv, pk_send, rw_recv, y_send, y_recv,
           op_send, pr_recv, rs_send, rs_recv, fin_send, out_recv, g_sem, free):
    ag, pk, rw = (ag0, ag1, ag2, ag3), (pk0, pk1), (rw0, rw1, rw2, rw3)
    py, act = (py0, py1), (act0, act1)
    op, pr = (op0, op1), (pr0, pr1, pr2, pr3)
    rs, first, fin = (rs0, rs1), (first0, first1), (fin0, fin1, fin2, fin3)
    sources, results = (tok, cot), (out, gtok)
    R = S * CAP * ROWS
    SLICE = CHUNKS * ROWS
    seq, y = lax.axis_index("seq"), lax.axis_index("ffn")
    z, s = seq // S, seq % S
    up_z, down_z = lax.rem(z + 1, Z), lax.rem(z + Z - 1, Z)
    toward = (up_z, down_z)
    hops = ((Z // 2, Z - 1 - Z // 2), (Z - 1 - Z // 2, Z // 2))

    def mate(d):
        return lax.rem(s + d, S)

    def in_plane(t):
        return (z * S + t, y)

    def along_z(direction):
        return (toward[direction] * S + s, y)

    def across_y(d):
        return (seq, lax.rem(y + d, Y))

    def each_mate(fn):
        def step(d, carry):
            fn(mate(d))
            return carry
        lax.fori_loop(1, S, step, 0)

    def settle(ref, sem):
        pltpu.make_async_copy(ref, ref, sem).wait()

    def spread(u):
        source, k = sources[u % 2], u // 2

        def piece(t):
            return source.at[pl.ds(pl.multiple_of(t * SLICE + k * ROWS, ROWS), ROWS)]

        def go(t):
            pltpu.make_async_remote_copy(
                src_ref=piece(t), dst_ref=ag[u].at[z * S + s], send_sem=sp_send.at[u], recv_sem=sp_recv.at[u],
                device_id=in_plane(t), device_id_type=MESH).start()
        each_mate(go)
        pltpu.make_async_copy(piece(s), ag[u].at[z * S + s], sp_recv.at[u]).start()

    def ag_copy(u, direction, hop):
        block = lax.rem(z + Z - hop + 1, Z) if direction == 0 else lax.rem(z + hop - 1, Z)
        ref = ag[u].at[pl.ds(block * S, S)]
        return pltpu.make_async_remote_copy(
            src_ref=ref, dst_ref=ref, send_sem=ag_send.at[u, direction, hop - 1],
            recv_sem=ag_recv.at[u, direction, hop - 1], device_id=along_z(direction), device_id_type=MESH)

    def ag_start(u):
        settle(ag[u].at[pl.ds(z * S, S)], sp_recv.at[u])
        for direction in range(2):
            ag_copy(u, direction, 1).start()

    def ag_forward(u, hop):
        for direction in range(2):
            if hop <= hops[u % 2][direction]:
                ag_copy(u, direction, hop - 1).wait_recv()
                ag_copy(u, direction, hop).start()

    def ag_finish(u):
        for direction in range(2):
            ag_copy(u, direction, hops[u % 2][direction]).wait_recv()

    def pack(u):
        a = u % 2
        if u >= 2:
            settle(pk[a].at[pl.ds(0, S - 1)], pk_send.at[u - 2])

        def go(t):
            for j in range(CAP):
                pk[a][t, j] = ag[u][slots[t * CAP + j]]
            pltpu.make_async_remote_copy(
                src_ref=pk[a].at[t], dst_ref=rw[u].at[s], send_sem=pk_send.at[u], recv_sem=rw_recv.at[u],
                device_id=in_plane(t), device_id_type=MESH).start()
        each_mate(go)
        for j in range(CAP):
            rw[u][s, j] = ag[u][slots[s * CAP + j]]

    def rows_ready(u):
        settle(rw[u].at[pl.ds(0, S - 1)], rw_recv.at[u])

    def feature_loop(width, fn):
        def step(b, carry):
            fn(pl.ds(pl.multiple_of(b * width, width), width))
            return carry
        lax.fori_loop(0, W // width, step, 0)

    def wide(ref, columns):
        return ref[:, :, :, columns].reshape(R, columns.size)

    def split(rows):
        return rows.reshape(Y, R // Y, U)

    def up_and_gate(k):
        if k:
            settle(part.at[pl.ds(0, Y - 1)], y_send.at[k - 1, 0])
        part[...] = jnp.zeros_like(part)

        def step(columns):
            x = wide(rw[2 * k], columns)
            part[:, 0] += split(dot(x, wu[columns, :], (1, 0)))
            part[:, 1] += split(dot(x, wg[columns, :], (1, 0)))
        feature_loop(min(512, W), step)

    def hidden_grad(k):
        def step(columns):
            x = wide(rw[2 * k + 1], columns)
            part[:, 2] += split(dot(x, wd[:, columns], (1, 1)))
        feature_loop(min(512, W), step)

    def sum_send(k):
        for d in range(1, Y):
            pltpu.make_async_remote_copy(
                src_ref=part.at[lax.rem(y + d, Y)], dst_ref=py[k].at[d - 1], send_sem=y_send.at[k, 0],
                recv_sem=y_recv.at[k, 0], device_id=across_y(d), device_id_type=MESH).start()

    def activate(k):
        settle(py[k], y_recv.at[k, 0])
        total = [part[y, i] for i in range(3)]
        for d in range(Y - 1):
            total = [total[i] + py[k][d, i] for i in range(3)]
        mask = row_mask[...]
        rectified = jnp.maximum(total[1], 0.0)
        square = rectified * rectified
        grad = total[2] * mask
        act[k][y, 0] = (square * total[0] * mask).astype(BF16)
        act[k][y, 1] = (grad * square).astype(BF16)
        act[k][y, 2] = (grad * total[0] * 2.0 * rectified).astype(BF16)
        for d in range(1, Y):
            pltpu.make_async_remote_copy(
                src_ref=act[k].at[y], dst_ref=act[k].at[y], send_sem=y_send.at[k, 1],
                recv_sem=y_recv.at[k, 1], device_id=across_y(d), device_id_type=MESH).start()

    def act_ready(k):
        settle(act[k].at[pl.ds(0, Y - 1)], y_recv.at[k, 1])

    def activation(k, i):
        return act[k][:, i].reshape(R, U)

    def give_back(u):
        a = u % 2

        def go(t):
            pltpu.make_async_remote_copy(
                src_ref=op[a].at[t], dst_ref=pr[u].at[s], send_sem=op_send.at[u], recv_sem=pr_recv.at[u],
                device_id=in_plane(t), device_id_type=MESH).start()
        each_mate(go)
        pltpu.make_async_copy(op[a].at[s], pr[u].at[s], pr_recv.at[u]).start()

    def down(k):
        u = 2 * k
        if k:
            settle(op[0].at[pl.ds(0, S - 1)], op_send.at[u - 2])

        def step(columns):
            product = dot(activation(k, 0), wd[:, columns], (1, 0))
            op[0][:, :, :, columns] = product.astype(BF16).reshape(S, CAP, ROWS, columns.size)
        feature_loop(min(512, W), step)
        give_back(u)

    def back(k):
        u = 2 * k + 1
        if k:
            settle(op[1].at[pl.ds(0, S - 1)], op_send.at[u - 2])

        def step(columns):
            product = dot(activation(k, 1), wu[columns, :], (1, 1))
            product = product + dot(activation(k, 2), wg[columns, :], (1, 1))
            op[1][:, :, :, columns] = product.astype(BF16).reshape(S, CAP, ROWS, columns.size)
        feature_loop(min(512, W), step)
        give_back(u)

    def collected(u):
        settle(pr[u], pr_recv.at[u])

    def plane_sum(u, target, columns):
        pick = sel[pl.ds(pl.multiple_of(target * (S * ROWS), S * ROWS), S * ROWS), :]
        return dot(pick, wide(pr[u], columns), (1, 0)).reshape(S, ROWS, columns.size)

    def slot_of(a, direction, hop):
        return hop - 1 + (hops[a][0] if direction else 0)

    def rs_copy(u, direction, hop):
        a = u % 2
        source = first[a].at[direction] if hop == 1 else rs[a].at[slot_of(a, direction, hop - 1)]
        return pltpu.make_async_remote_copy(
            src_ref=source, dst_ref=rs[a].at[slot_of(a, direction, hop)],
            send_sem=rs_send.at[u, direction, hop - 1], recv_sem=rs_recv.at[u, direction, hop - 1],
            device_id=along_z(direction), device_id_type=MESH)

    def release(u, direction):
        if u < 2:
            pl.semaphore_signal(free.at[u, direction], inc=1, device_id=along_z(1 - direction), device_id_type=MESH)

    def rs_step(u, direction, hop):
        a = u % 2
        last = hops[a][direction]
        if hop > last:
            return
        far = last - hop + 1
        target = lax.rem(z + far, Z) if direction == 0 else lax.rem(z + Z - far, Z)
        if hop == 1:
            if u >= 2:
                rs_copy(u - 2, direction, 1).wait_send()

            def step(columns):
                first[a][direction, :, :, columns] = plane_sum(u, target, columns).astype(BF16)
        else:
            if hop > 2:
                rs_copy(u, direction, hop - 1).wait_send()
                release(u, direction)
            rs_copy(u, direction, hop - 1).wait_recv()
            at = slot_of(a, direction, hop - 1)

            def step(columns):
                total = rs[a][at, :, :, columns].astype(F32) + plane_sum(u, target, columns)
                rs[a][at, :, :, columns] = total.astype(BF16)
        feature_loop(min(512, W), step)
        if u >= 2:
            pl.semaphore_wait(free.at[u - 2, direction], 1)
        rs_copy(u, direction, hop).start()

    def rs_both(u, hop):
        for direction in range(2):
            rs_step(u, direction, hop)

    def finish(u):
        a, k = u % 2, u // 2
        ends = []
        for direction in range(2):
            last = hops[a][direction]
            if last > 1:
                rs_copy(u, direction, last).wait_send()
                release(u, direction)
            rs_copy(u, direction, last).wait_recv()
            ends.append(slot_of(a, direction, last))

        def step(columns):
            total = plane_sum(u, z, columns)
            for at in ends:
                total = total + rs[a][at, :, :, columns].astype(F32)
            fin[u][:, :, columns] = total.astype(BF16)
        feature_loop(min(512, W), step)
        for direction in range(2):
            release(u, direction)
        place = results[a].at[pl.ds(pl.multiple_of(s * SLICE + k * ROWS, ROWS), ROWS)]

        def go(t):
            pltpu.make_async_remote_copy(
                src_ref=fin[u].at[t], dst_ref=place, send_sem=fin_send.at[u], recv_sem=out_recv.at[u],
                device_id=in_plane(t), device_id_type=MESH).start()
        each_mate(go)
        pltpu.make_async_copy(fin[u].at[s], place, out_recv.at[u]).start()

    def token_weight_grad(i, buffer, target):
        width = min(256, W)

        def step(b, carry):
            columns = pl.ds(pl.multiple_of(b * width, width), width)
            total = dot(wide(rw[0], columns), activation(0, i), (0, 0))
            total = total + dot(wide(rw[2], columns), activation(1, i), (0, 0))
            buffer[columns, :] = (total * grad_scale).astype(BF16)
            return carry
        lax.fori_loop(0, W // width, step, 0)
        pltpu.make_async_copy(buffer, target, g_sem.at[i]).start()

    def down_weight_grad(buffer, target):
        width = min(256, W)

        def step(columns):
            total = dot(activation(0, 0), wide(rw[1], columns), (0, 0))
            total = total + dot(activation(1, 0), wide(rw[3], columns), (0, 0))
            buffer[:, columns] = (total * grad_scale).astype(BF16)
        feature_loop(width, step)
        pltpu.make_async_copy(buffer, target, g_sem.at[0]).start()

    grad_scale = 1.0 / (S * SLICE)
    weights = [pltpu.make_async_copy(wu_in, wu, w_sem.at[0]), pltpu.make_async_copy(wg_in, wg, w_sem.at[1]),
               pltpu.make_async_copy(wd_in, wd, w_sem.at[2])]
    for copy in weights:
        copy.start()

    barrier = pltpu.get_barrier_semaphore()

    def greet(device):
        pl.semaphore_signal(barrier, inc=1, device_id=device, device_id_type=MESH)
    each_mate(lambda t: greet(in_plane(t)))
    for direction in range(2):
        greet(along_z(direction))
    for d in range(1, Y):
        greet(across_y(d))
    pl.semaphore_wait(barrier, S - 1 + 2 + Y - 1)

    for u in range(4):
        spread(u)
    ag_start(0)
    ag_start(1)

    def select_rows(g, carry):
        row = lax.broadcasted_iota(jnp.int32, (ROWS, R), 0)
        column = lax.broadcasted_iota(jnp.int32, (ROWS, R), 1)
        hit = (column_group[...] == g) & (lax.rem(column, ROWS) == row)
        sel[pl.ds(pl.multiple_of(g * ROWS, ROWS), ROWS), :] = jnp.where(hit, 1.0, 0.0).astype(BF16)
        return carry
    lax.fori_loop(0, Z * S, select_rows, 0)
    for copy in weights:
        copy.wait()

    far = max(hops[0])
    for hop in range(2, far + 1):
        ag_forward(0, hop)
        ag_forward(1, hop)
    ag_start(2)
    ag_start(3)

    def chunk_steps(k):
        t, c = 2 * k, 2 * k + 1
        return [
            lambda: (ag_finish(t), pack(t), ag_finish(c), pack(c)),
            lambda: (rows_ready(t), up_and_gate(k)),
            lambda: (rows_ready(c), hidden_grad(k), sum_send(k)),
            lambda: activate(k),
            lambda: (act_ready(k), down(k)),
            lambda: back(k),
        ]

    def weave(main, beside):
        n = max(len(main), len(beside))
        for i in range(n):
            if i < len(main):
                main[i]()
            if i < len(beside):
                beside[i]()

    weave(chunk_steps(0), [functools.partial(ag_forward, u, hop) for hop in range(2, far + 1) for u in (2, 3)])
    for u in (0, 1):
        collected(u)
        rs_both(u, 1)
    weave(chunk_steps(1), [functools.partial(rs_both, u, hop) for hop in range(2, far + 1) for u in (0, 1)])
    finish(0)
    finish(1)
    for u in (2, 3):
        collected(u)
        rs_both(u, 1)
    weave([functools.partial(token_weight_grad, 1, wu, gu_out), functools.partial(token_weight_grad, 2, wg, gg_out),
           functools.partial(down_weight_grad, wd, gd_out)],
          [functools.partial(rs_both, u, hop) for hop in range(2, far + 1) for u in (2, 3)])
    finish(2)
    finish(3)

    for u in range(4):
        a, k = u % 2, u // 2
        settle(sources[a].at[pl.ds(0, (S - 1) * ROWS)], sp_send.at[u])
        for direction in range(2):
            for hop in range(1, hops[a][direction] + 1):
                ag_copy(u, direction, hop).wait_send()
        settle(fin[u].at[pl.ds(0, S - 1)], fin_send.at[u])
        settle(results[a].at[pl.ds(0, S * ROWS)], out_recv.at[u])
    for u in (2, 3):
        a = u % 2
        settle(pk[a].at[pl.ds(0, S - 1)], pk_send.at[u])
        settle(op[a].at[pl.ds(0, S - 1)], op_send.at[u])
        for direction in range(2):
            rs_copy(u, direction, 1).wait_send()
    settle(part.at[pl.ds(0, Y - 1)], y_send.at[1, 0])
    for k in range(CHUNKS):
        settle(act[k].at[pl.ds(0, Y - 1)], y_send.at[k, 1])
    for i, (buffer, target) in enumerate(((wd, gd_out), (wu, gu_out), (wg, gg_out))):
        pltpu.make_async_copy(buffer, target, g_sem.at[i]).wait()


def body(tokens, cotangent, block_masks, w_up, w_gate, w_down):
    owners, Y = lax.axis_size("seq"), lax.axis_size("ffn")
    S, Z = PLANE, owners // PLANE
    _, group_len, W = tokens.shape
    groups = block_masks.shape[0]
    U = w_up.shape[1]
    owner_blocks = U // BLK
    R = S * CAP * ROWS
    my_owner = lax.axis_index("seq")
    first_owner = (my_owner // S) * S
    mine = lax.dynamic_slice_in_dim(block_masks, first_owner * owner_blocks, S * owner_blocks, 1)
    active = jnp.max(mine.reshape(groups, S, owner_blocks), axis=2).T
    ordinal = jnp.cumsum(active, axis=1) - 1
    slot_ids = jnp.arange(CAP, dtype=jnp.int32)
    picked = (ordinal[:, None, :] == slot_ids[None, :, None]) & (active[:, None, :] > 0)
    group_ids = jnp.arange(groups, dtype=jnp.int32)
    slot_group = jnp.sum(jnp.where(picked, group_ids, 0), axis=2).reshape(-1)
    held_group = jnp.where(jnp.any(picked, axis=2).reshape(-1), slot_group, -1)
    column_group = jnp.repeat(held_group, ROWS).reshape(1, R)
    my_picked = lax.dynamic_index_in_dim(picked, my_owner % S, 0, keepdims=False)
    my_columns = lax.dynamic_slice_in_dim(block_masks, my_owner * owner_blocks, owner_blocks, 1)
    block_live = jnp.sum(jnp.where(my_picked[:, :, None], my_columns[None], 0), axis=1).astype(F32)
    unit_live = jnp.repeat(block_live, BLK, axis=1)
    quarter = R // Y
    row_mask = jnp.broadcast_to(
        unit_live[None, :, None, :], (quarter // (CAP * ROWS), CAP, ROWS, U)).reshape(quarter, U)

    hbm, vmem = pl.BlockSpec(memory_space=pl.ANY), pl.BlockSpec(memory_space=pltpu.VMEM)
    half = Z // 2
    rows = pltpu.VMEM((S, CAP, ROWS, W), BF16)
    gathered = pltpu.VMEM((Z * S, ROWS, W), BF16)
    dma = pltpu.SemaphoreType.DMA
    scratch = (
        [gathered] * 4 + [rows] * 2 + [rows] * 4
        + [pltpu.VMEM((W, U), BF16)] * 2 + [pltpu.VMEM((U, W), BF16)]
        + [pltpu.VMEM((Y, 3, quarter, U), F32)]
        + [pltpu.VMEM((Y - 1, 3, quarter, U), F32)] * 2
        + [pltpu.VMEM((Y, 3, quarter, U), BF16)] * 2
        + [rows] * 2 + [rows] * 4
        + [pltpu.VMEM((Z - 1, S, ROWS, W), BF16)] * 2
        + [pltpu.VMEM((2, S, ROWS, W), BF16)] * 2
        + [pltpu.VMEM((S, ROWS, W), BF16)] * 4
        + [pltpu.VMEM((Z * S * ROWS, R), BF16)]
        + [
            dma((3,)), dma((4,)), dma((4,)), dma((4, 2, half)), dma((4, 2, half)), dma((4,)), dma((4,)),
            dma((2, 2)), dma((2, 2)), dma((4,)), dma((4,)), dma((4, 2, half)), dma((4, 2, half)), dma((4,)),
            dma((4,)), dma((3,)), pltpu.SemaphoreType.REGULAR((2, 2)),
        ]
    )
    shapes = (
        jax.ShapeDtypeStruct((group_len, W), BF16), jax.ShapeDtypeStruct((group_len, W), BF16),
        jax.ShapeDtypeStruct((W, U), BF16), jax.ShapeDtypeStruct((W, U), BF16), jax.ShapeDtypeStruct((U, W), BF16),
    )
    outputs, grad_tokens, grad_up, grad_gate, grad_down = pl.pallas_call(
        functools.partial(kernel, Z, S, Y, W, U),
        out_shape=shapes,
        in_specs=[pl.BlockSpec(memory_space=pltpu.SMEM), vmem, vmem] + [hbm] * 5,
        out_specs=[hbm] * 5,
        scratch_shapes=scratch,
        compiler_params=pltpu.CompilerParams(
            collective_id=0, has_side_effects=True, vmem_limit_bytes=63 * 1024 * 1024),
        cost_estimate=pl.CostEstimate(flops=18 * CHUNKS * R * W * U, bytes_accessed=10 * 2**20, transcendentals=0),
    )(slot_group, column_group, row_mask, tokens.reshape(group_len, W), cotangent.reshape(group_len, W),
      w_up, w_gate, w_down)
    return outputs[None], grad_tokens[None], grad_up, grad_gate, grad_down


def solution(mesh):
    in_specs = (
        P("seq", None, "ffn"),
        P("seq", None, "ffn"),
        P(),
        P("ffn", "seq"),
        P("ffn", "seq"),
        P("seq", "ffn"),
    )
    out_specs = (
        P("seq", None, "ffn"),
        P("seq", None, "ffn"),
        P("ffn", "seq"),
        P("ffn", "seq"),
        P("seq", "ffn"),
    )
    return jax.shard_map(body, mesh=mesh, in_specs=in_specs, out_specs=out_specs, check_vma=False)
```

time: 833 us -> 386 us (0.46); the launches traced: 824 us -> 386 us
  waiting for transfers between devices: 556 us -> 0 us
  Pallas kernels: 0 us -> 373 us
  local copies, waits for them, and re-layouts: 115 us -> 11.3 us
  starting transfers between devices: 76.4 us -> 0 us
  matrix products: 42.2 us -> 0 us
  other arithmetic: 19 us -> 0.87 us
  between operations: 14.8 us -> 0.73 us
    all_to_all x8 -> x0, waiting for transfers between devices: 490 us -> none  [the longest x1 174 us: body(): lax.all_to_all(input_part, 'seq', split_axis=1, concat_axis=0, tiled=True)]
    pallas_call x0 -> x1, Pallas kernels: none -> 373 us  [body(): pl.pallas_call(functools.partial(kernel, Z, S, Y, W, U), out_shape=shapes...]
    all_to_all x8 -> x0, starting transfers between devices: 76.4 us -> none  [the longest x1 13.6 us: body(): lax.all_to_all(tokens, 'seq', split_axis=1, concat_axis=0, tiled=True)]
    psum x1 -> x0, waiting for transfers between devices: 65.7 us -> none  [body(): up_full, gate_full = lax.psum((up_part, gate_part), 'ffn')]
    dot_general x12 -> x0, matrix products: 42.2 us -> none  [the longest x2 21.2 us: settle(): jnp.einsum('sg,spw->gpw', select_map, returned, precision=lax.Precision.H...]
    all_to_all x8 -> x0, local copies, waits for them, and re-layouts: 30.2 us -> none  [the longest x2 8.5 us: body(): lax.all_to_all(tokens, 'seq', split_axis=1, concat_axis=0, tiled=True)]
    gather x4 -> x0, local copies, waits for them, and re-layouts: 30.1 us -> none  [the longest x2 15.1 us: body(): packed_cotan = spread_cotan[lookup]]
    reshape x4 -> x2, local copies, waits for them, and re-layouts: 26.1 us -> 0.17 us  [the longest x1 0.09 us: body(): held_group = jnp.where(jnp.any(picked, axis=2).reshape(-1), slot_group, -1)]
  transfers between devices with their start and end apart: 9 -> 0, of which waited for: 8 -> 0; matrix products, arithmetic and copies ran while one was open for 16% -> 0% of each run, Pallas kernels for 0% -> 0%
where the time goes in v1:
time: 386 us
  Pallas kernels  373 us (97%)
  local copies, waits for them, and re-layouts  11.3 us (3%)
    pallas_call x1, Pallas kernels, body(): pl.pallas_call(functools.partial(kernel, Z, S, Y, W, U), out_shape=shapes...  373 us
    unnamed x20, local copies, waits for them, and re-layouts  9.56 us

profile of v1, /device:TPU:1, one launch (start us, length us, event | category | flops | bytes accessed | tf_op | source)
XLA Modules:
  0.0 385.9 jit_solution(12332195408828623055)
XLA Ops:
  0.6 0.0 copy-start
  0.7 0.7 copy-done
  1.4 0.1 constant_dynamic-slice_fusion
  1.5 0.1 copy.21
  1.5 0.1 constant_dynamic-slice_fusion.1
  1.6 0.1 copy.24
  1.7 0.2 reduce_window_sum.11
  2.0 0.2 fusion.1
  2.2 0.1 reshape.43
  2.3 0.2 select_reduce_fusion
  2.5 0.1 reshape.42.slots
  2.6 0.0 copy-start.5
  2.6 0.5 copy-done.5
  3.1 0.1 select_reduce_fusion.1
  3.3 0.1 broadcast_bitcast_fusion
  3.3 0.1 broadcast_in_dim.61
  3.4 0.7 reshape_reshape.3.column_group
  4.1 0.6 broadcast_in_dim.68
  4.7 373.0 %shard_map.101 = (bf16[256,2048]{1,0:T(8,128)(2,1)}, bf16[256,2048]{1,0:T(8,128)(2,1)}, bf16[2048,256]{1,0:T(8,128)(2,1)}, bf16[2048,256]{1,0:T(8,128)(2,1)}, bf16[256,2048]{1,0:T(8,128)(2,1)}) custom-call(s32[24]{0:T(128)} %copy-done.5, s32[1,384]{1,0:T(1,128)} %reshape_reshape.3.column_group, f32[96,256]{1,0:T(8,128)} %bitcast.17, ...), custom_call_target="tpu_custom_call" | custom-call | flops 7247757312 | bytes 10485760 | tf_op jit(solution)/shard_map/pallas_call | solution.py:459
  377.8 0.0 copy-start.4
  377.8 2.4 copy.33
  380.2 0.0 copy-done.4
  380.2 0.0 copy-start.3
  380.2 1.0 copy.34
  381.1 0.6 copy-done.3
  381.8 0.0 copy-start.2
  381.8 1.0 copy.35
  382.7 0.6 copy-done.2
  383.4 0.0 copy-start.1
  383.4 1.0 copy.36
  384.3 0.6 copy-done.1
  385.0 1.0 copy.37
  (7 shorter events, 0.1 us)
Async XLA Ops:
  0.6 0.8 copy-start
  2.6 0.5 copy-start.5
  377.8 2.4 copy-start.4
  380.2 1.6 copy-start.3
  381.8 1.6 copy-start.2
  383.4 1.6 copy-start.1

commit v2 on v1

--- a/solution.py
+++ b/solution.py
@@ -20,16 +20,34 @@
     return lax.dot_general(left, right, (((dims[0],), (dims[1],)), ((), ())), preferred_element_type=F32)
 
 
-def kernel(Z, S, Y, W, U, slots, column_group, row_mask, tok, cot, wu_in, wg_in, wd_in,
+def offsets(caps, hops, S):
+    at, table = S, []
+    for direction in range(2):
+        row = []
+        for count in caps[hops[direction]]:
+            row.append(at)
+            at += count
+        table.append(row)
+    return table, at
+
+
+def hop_counts(Z):
+    far, near = Z // 2, Z - 1 - Z // 2
+    return ((far, near), (near, far))
+
+
+def kernel(Z, S, Y, W, U, caps, slots, sums, orders, column_group, row_mask, tok, cot, wu_in, wg_in, wd_in,
            out, gtok, gu_out, gg_out, gd_out,
-           ag0, ag1, ag2, ag3, pk0, pk1, rw0, rw1, rw2, rw3, wu, wg, wd, part, py0, py1, act0, act1,
-           op0, op1, pr0, pr1, pr2, pr3, rs0, rs1, first0, first1, fin0, fin1, fin2, fin3, sel,
+           ag0, ag1, ag2, ag3, so0, so1, so2, so3, pk0, pk1, rw0, rw1, rw2, rw3, wu, wg, wd, part, py0, py1, act0, act1,
+           op0, op1, pr0, pr1, pr2, pr3, rs0, rs1, f00, f01, f10, f11, fin0, fin1, fin2, fin3, sel,
+           sort0, sort1, sort2, sort3,
            w_sem, sp_send, sp_recv, ag_send, ag_recv, pk_send, rw_recv, y_send, y_recv,
            op_send, pr_recv, rs_send, rs_recv, fin_send, out_recv, g_sem, free):
     ag, pk, rw = (ag0, ag1, ag2, ag3), (pk0, pk1), (rw0, rw1, rw2, rw3)
     py, act = (py0, py1), (act0, act1)
     op, pr = (op0, op1), (pr0, pr1, pr2, pr3)
-    rs, first, fin = (rs0, rs1), (first0, first1), (fin0, fin1, fin2, fin3)
+    rs, first, fin = (rs0, rs1), ((f00, f01), (f10, f11)), (fin0, fin1, fin2, fin3)
+    sorted_rows, sort = ((so0, so1), (so2, so3)), ((sort0, sort1), (sort2, sort3))
     sources, results = (tok, cot), (out, gtok)
     R = S * CAP * ROWS
     SLICE = CHUNKS * ROWS
@@ -37,7 +55,8 @@
     z, s = seq // S, seq % S
     up_z, down_z = lax.rem(z + 1, Z), lax.rem(z + Z - 1, Z)
     toward = (up_z, down_z)
-    hops = ((Z // 2, Z - 1 - Z // 2), (Z - 1 - Z // 2, Z // 2))
+    hops = hop_counts(Z)
+    blocks = [offsets(caps, hops[a], S)[0] for a in range(2)]
 
     def mate(d):
         return lax.rem(s + d, S)
@@ -68,21 +87,36 @@
 
         def go(t):
             pltpu.make_async_remote_copy(
-                src_ref=piece(t), dst_ref=ag[u].at[z * S + s], send_sem=sp_send.at[u], recv_sem=sp_recv.at[u],
+                src_ref=piece(t), dst_ref=ag[u].at[s], send_sem=sp_send.at[u], recv_sem=sp_recv.at[u],
                 device_id=in_plane(t), device_id_type=MESH).start()
         each_mate(go)
-        pltpu.make_async_copy(piece(s), ag[u].at[z * S + s], sp_recv.at[u]).start()
+        pltpu.make_async_copy(piece(s), ag[u].at[s], sp_recv.at[u]).start()
+
+    def arrivals(a, direction, hop, count):
+        return pl.ds(blocks[a][direction][hop - 1], count)
 
     def ag_copy(u, direction, hop):
-        block = lax.rem(z + Z - hop + 1, Z) if direction == 0 else lax.rem(z + hop - 1, Z)
-        ref = ag[u].at[pl.ds(block * S, S)]
+        a = u % 2
+        count = caps[hops[a][direction]][hop - 1]
+        source = sorted_rows[a][direction] if hop == 1 else ag[u].at[arrivals(a, direction, hop - 1, count)]
         return pltpu.make_async_remote_copy(
-            src_ref=ref, dst_ref=ref, send_sem=ag_send.at[u, direction, hop - 1],
-            recv_sem=ag_recv.at[u, direction, hop - 1], device_id=along_z(direction), device_id_type=MESH)
+            src_ref=source, dst_ref=ag[u].at[arrivals(a, direction, hop, count)],
+            send_sem=ag_send.at[u, direction, hop - 1], recv_sem=ag_recv.at[u, direction, hop - 1],
+            device_id=along_z(direction), device_id_type=MESH)
 
     def ag_start(u):
-        settle(ag[u].at[pl.ds(z * S, S)], sp_recv.at[u])
-        for direction in range(2):
+        a = u % 2
+        settle(ag[u].at[pl.ds(0, S)], sp_recv.at[u])
+        for direction in range(2):
+            target = sorted_rows[a][direction]
+            if u >= 2:
+                ag_copy(u - 2, direction, 1).wait_send()
+
+            def step(columns):
+                own = ag[u][0:S, :, columns].reshape(S * ROWS, columns.size)
+                moved = dot(sort[a][direction][...], own, (1, 0)).astype(BF16)
+                target[:, :, columns] = moved.reshape(target.shape[0], ROWS, columns.size)
+            feature_loop(min(512, W), step)
             ag_copy(u, direction, 1).start()
 
     def ag_forward(u, hop):
@@ -102,13 +136,13 @@
 
         def go(t):
             for j in range(CAP):
-                pk[a][t, j] = ag[u][slots[t * CAP + j]]
+                pk[a][t, j] = ag[u][slots[a, t * CAP + j]]
             pltpu.make_async_remote_copy(
                 src_ref=pk[a].at[t], dst_ref=rw[u].at[s], send_sem=pk_send.at[u], recv_sem=rw_recv.at[u],
                 device_id=in_plane(t), device_id_type=MESH).start()
         each_mate(go)
         for j in range(CAP):
-            rw[u][s, j] = ag[u][slots[s * CAP + j]]
+            rw[u][s, j] = ag[u][slots[a, s * CAP + j]]
 
     def rows_ready(u):
         settle(rw[u].at[pl.ds(0, S - 1)], rw_recv.at[u])
@@ -207,18 +241,44 @@
     def collected(u):
         settle(pr[u], pr_recv.at[u])
 
-    def plane_sum(u, target, columns):
-        pick = sel[pl.ds(pl.multiple_of(target * (S * ROWS), S * ROWS), S * ROWS), :]
-        return dot(pick, wide(pr[u], columns), (1, 0)).reshape(S, ROWS, columns.size)
-
-    def slot_of(a, direction, hop):
-        return hop - 1 + (hops[a][0] if direction else 0)
+    sum_rows = [S * ROWS]
+    sum_at = []
+    for a in range(2):
+        sum_at.append([])
+        for direction in range(2):
+            row = []
+            for count in caps[hops[a][direction]]:
+                row.append(sum_rows[0])
+                sum_rows[0] += count * ROWS
+            sum_at[a].append(row)
+
+    def plane_sum(u, direction, far, columns):
+        a = u % 2
+        at, count = (0, S) if far == 0 else (sum_at[a][direction][far - 1], caps[hops[a][direction]][far - 1])
+        pick = sel[at:at + count * ROWS, :]
+        return dot(pick, wide(pr[u], columns), (1, 0)).reshape(count, ROWS, columns.size)
+
+    room = []
+    for a in range(2):
+        at, table = 0, []
+        for direction in range(2):
+            row, counts = [], caps[hops[a][direction]]
+            for hop in range(1, len(counts) + 1):
+                row.append(at)
+                at += counts[max(len(counts) - hop, 1) - 1]
+            table.append(row)
+        room.append(table)
+
+    def received(a, direction, hop, count):
+        return rs[a].at[pl.ds(room[a][direction][hop - 1], count)]
 
     def rs_copy(u, direction, hop):
         a = u % 2
-        source = first[a].at[direction] if hop == 1 else rs[a].at[slot_of(a, direction, hop - 1)]
+        counts = caps[hops[a][direction]]
+        count = counts[len(counts) - hop]
+        source = first[a][direction] if hop == 1 else received(a, direction, hop - 1, count)
         return pltpu.make_async_remote_copy(
-            src_ref=source, dst_ref=rs[a].at[slot_of(a, direction, hop)],
+            src_ref=source, dst_ref=received(a, direction, hop, count),
             send_sem=rs_send.at[u, direction, hop - 1], recv_sem=rs_recv.at[u, direction, hop - 1],
             device_id=along_z(direction), device_id_type=MESH)
 
@@ -232,23 +292,26 @@
         if hop > last:
             return
         far = last - hop + 1
-        target = lax.rem(z + far, Z) if direction == 0 else lax.rem(z + Z - far, Z)
         if hop == 1:
             if u >= 2:
                 rs_copy(u - 2, direction, 1).wait_send()
 
             def step(columns):
-                first[a][direction, :, :, columns] = plane_sum(u, target, columns).astype(BF16)
+                first[a][direction][:, :, columns] = plane_sum(u, direction, far, columns).astype(BF16)
         else:
             if hop > 2:
                 rs_copy(u, direction, hop - 1).wait_send()
                 release(u, direction)
             rs_copy(u, direction, hop - 1).wait_recv()
-            at = slot_of(a, direction, hop - 1)
+            old = caps[last][far]
+            arrived = received(a, direction, hop - 1, old)
+            fresh = rs[a].at[pl.ds(room[a][direction][hop - 2] + old, caps[last][far - 1] - old)]
 
             def step(columns):
-                total = rs[a][at, :, :, columns].astype(F32) + plane_sum(u, target, columns)
-                rs[a][at, :, :, columns] = total.astype(BF16)
+                total = plane_sum(u, direction, far, columns)
+                arrived[:, :, columns] = (arrived[:, :, columns].astype(F32) + total[:old]).astype(BF16)
+                if caps[last][far - 1] > old:
+                    fresh[:, :, columns] = total[old:].astype(BF16)
         feature_loop(min(512, W), step)
         if u >= 2:
             pl.semaphore_wait(free.at[u - 2, direction], 1)
@@ -267,12 +330,13 @@
                 rs_copy(u, direction, last).wait_send()
                 release(u, direction)
             rs_copy(u, direction, last).wait_recv()
-            ends.append(slot_of(a, direction, last))
+            ends.append(received(a, direction, last, caps[last][0]))
 
         def step(columns):
-            total = plane_sum(u, z, columns)
-            for at in ends:
-                total = total + rs[a][at, :, :, columns].astype(F32)
+            total = plane_sum(u, 0, 0, columns)
+            for direction in range(2):
+                arrived = ends[direction][:, :, columns].reshape(-1, columns.size)
+                total = total + dot(sort[1 - a][1 - direction][...], arrived, (0, 0)).reshape(S, ROWS, columns.size)
             fin[u][:, :, columns] = total.astype(BF16)
         feature_loop(min(512, W), step)
         for direction in range(2):
@@ -327,16 +391,23 @@
 
     for u in range(4):
         spread(u)
+    for a in range(2):
+        for direction in range(2):
+            for r in range(caps[hops[a][direction]][0]):
+                row = lax.broadcasted_iota(jnp.int32, (ROWS, S * ROWS), 0)
+                column = lax.broadcasted_iota(jnp.int32, (ROWS, S * ROWS), 1)
+                hit = column == orders[2 * a + direction, r] * ROWS + row
+                sort[a][direction][r * ROWS:(r + 1) * ROWS, :] = jnp.where(hit, 1.0, 0.0).astype(BF16)
     ag_start(0)
     ag_start(1)
 
     def select_rows(g, carry):
         row = lax.broadcasted_iota(jnp.int32, (ROWS, R), 0)
         column = lax.broadcasted_iota(jnp.int32, (ROWS, R), 1)
-        hit = (column_group[...] == g) & (lax.rem(column, ROWS) == row)
+        hit = (column_group[...] == sums[g]) & (lax.rem(column, ROWS) == row)
         sel[pl.ds(pl.multiple_of(g * ROWS, ROWS), ROWS), :] = jnp.where(hit, 1.0, 0.0).astype(BF16)
         return carry
-    lax.fori_loop(0, Z * S, select_rows, 0)
+    lax.fori_loop(0, sum_rows[0] // ROWS, select_rows, 0)
     for copy in weights:
         copy.wait()
 
@@ -386,7 +457,7 @@
         a, k = u % 2, u // 2
         settle(sources[a].at[pl.ds(0, (S - 1) * ROWS)], sp_send.at[u])
         for direction in range(2):
-            for hop in range(1, hops[a][direction] + 1):
+            for hop in range(1 if k else 2, hops[a][direction] + 1):
                 ag_copy(u, direction, hop).wait_send()
         settle(fin[u].at[pl.ds(0, S - 1)], fin_send.at[u])
         settle(results[a].at[pl.ds(0, S * ROWS)], out_recv.at[u])
@@ -403,49 +474,63 @@
         pltpu.make_async_copy(buffer, target, g_sem.at[i]).wait()
 
 
-def body(tokens, cotangent, block_masks, w_up, w_gate, w_down):
-    owners, Y = lax.axis_size("seq"), lax.axis_size("ffn")
-    S, Z = PLANE, owners // PLANE
-    _, group_len, W = tokens.shape
-    groups = block_masks.shape[0]
-    U = w_up.shape[1]
-    owner_blocks = U // BLK
+def levels(Z, S):
+    far = Z // 2
+    full = {far: (S,) * far, Z - 1 - far: (S,) * (Z - 1 - far)}
+    if (Z, S) != (8, 8):
+        return [full]
+    return [{4: (7, 6, 5, 3), 3: (6, 5, 4)}, {4: (8, 7, 6, 4), 3: (7, 6, 4)}, full]
+
+
+def ffn(level, caps, Z, S, Y, U, held_group, slot_place, sum_orders, sort_orders, row_mask, tokens, cotangent,
+        w_up, w_gate, w_down):
+    group_len, W = tokens.shape
     R = S * CAP * ROWS
-    my_owner = lax.axis_index("seq")
-    first_owner = (my_owner // S) * S
-    mine = lax.dynamic_slice_in_dim(block_masks, first_owner * owner_blocks, S * owner_blocks, 1)
-    active = jnp.max(mine.reshape(groups, S, owner_blocks), axis=2).T
-    ordinal = jnp.cumsum(active, axis=1) - 1
-    slot_ids = jnp.arange(CAP, dtype=jnp.int32)
-    picked = (ordinal[:, None, :] == slot_ids[None, :, None]) & (active[:, None, :] > 0)
-    group_ids = jnp.arange(groups, dtype=jnp.int32)
-    slot_group = jnp.sum(jnp.where(picked, group_ids, 0), axis=2).reshape(-1)
-    held_group = jnp.where(jnp.any(picked, axis=2).reshape(-1), slot_group, -1)
+    quarter = R // Y
+    hops = hop_counts(Z)
+    start = [offsets(caps, hops[a], S) for a in range(2)]
+    slots = []
+    for a in range(2):
+        away, rank = slot_place[a]
+        first = jnp.asarray([0] + start[a][0][0] + start[a][0][1][::-1], jnp.int32)
+        slots.append(jnp.sum(jnp.where(away[:, None] == jnp.arange(Z)[None, :], first[None, :], 0), axis=1) + rank)
+    slots = jnp.stack(slots).astype(jnp.int32)
+    sums = [sum_orders[0]]
+    for a in range(2):
+        for direction in range(2):
+            for far, count in enumerate(caps[hops[a][direction]]):
+                sums.append(sum_orders[1][a][direction][far][:count])
+    sums = jnp.concatenate(sums).astype(jnp.int32)
     column_group = jnp.repeat(held_group, ROWS).reshape(1, R)
-    my_picked = lax.dynamic_index_in_dim(picked, my_owner % S, 0, keepdims=False)
-    my_columns = lax.dynamic_slice_in_dim(block_masks, my_owner * owner_blocks, owner_blocks, 1)
-    block_live = jnp.sum(jnp.where(my_picked[:, :, None], my_columns[None], 0), axis=1).astype(F32)
-    unit_live = jnp.repeat(block_live, BLK, axis=1)
-    quarter = R // Y
-    row_mask = jnp.broadcast_to(
-        unit_live[None, :, None, :], (quarter // (CAP * ROWS), CAP, ROWS, U)).reshape(quarter, U)
 
     hbm, vmem = pl.BlockSpec(memory_space=pl.ANY), pl.BlockSpec(memory_space=pltpu.VMEM)
+    smem = pl.BlockSpec(memory_space=pltpu.SMEM)
     half = Z // 2
     rows = pltpu.VMEM((S, CAP, ROWS, W), BF16)
-    gathered = pltpu.VMEM((Z * S, ROWS, W), BF16)
     dma = pltpu.SemaphoreType.DMA
+
+    def groups_of(count):
+        return pltpu.VMEM((count, ROWS, W), BF16)
+
+    def counts(a, direction):
+        return caps[hops[a][direction]]
+    ways = [(a, direction) for a in range(2) for direction in range(2)]
+    room = [sum(sum(counts(a, d)[max(len(counts(a, d)) - hop, 1) - 1] for hop in range(1, len(counts(a, d)) + 1))
+                for d in range(2)) for a in range(2)]
     scratch = (
-        [gathered] * 4 + [rows] * 2 + [rows] * 4
+        [groups_of(start[u % 2][1]) for u in range(4)]
+        + [groups_of(counts(a, d)[0]) for a, d in ways]
+        + [rows] * 2 + [rows] * 4
         + [pltpu.VMEM((W, U), BF16)] * 2 + [pltpu.VMEM((U, W), BF16)]
         + [pltpu.VMEM((Y, 3, quarter, U), F32)]
         + [pltpu.VMEM((Y - 1, 3, quarter, U), F32)] * 2
         + [pltpu.VMEM((Y, 3, quarter, U), BF16)] * 2
         + [rows] * 2 + [rows] * 4
-        + [pltpu.VMEM((Z - 1, S, ROWS, W), BF16)] * 2
-        + [pltpu.VMEM((2, S, ROWS, W), BF16)] * 2
-        + [pltpu.VMEM((S, ROWS, W), BF16)] * 4
-        + [pltpu.VMEM((Z * S * ROWS, R), BF16)]
+        + [groups_of(room[a]) for a in range(2)]
+        + [groups_of(counts(a, d)[-1]) for a, d in ways]
+        + [groups_of(S)] * 4
+        + [pltpu.VMEM((sums.shape[0] * ROWS, R), BF16)]
+        + [pltpu.VMEM((counts(a, d)[0] * ROWS, S * ROWS), BF16) for a, d in ways]
         + [
             dma((3,)), dma((4,)), dma((4,)), dma((4, 2, half)), dma((4, 2, half)), dma((4,)), dma((4,)),
             dma((2, 2)), dma((2, 2)), dma((4,)), dma((4,)), dma((4, 2, half)), dma((4, 2, half)), dma((4,)),
@@ -456,17 +541,114 @@
         jax.ShapeDtypeStruct((group_len, W), BF16), jax.ShapeDtypeStruct((group_len, W), BF16),
         jax.ShapeDtypeStruct((W, U), BF16), jax.ShapeDtypeStruct((W, U), BF16), jax.ShapeDtypeStruct((U, W), BF16),
     )
-    outputs, grad_tokens, grad_up, grad_gate, grad_down = pl.pallas_call(
-        functools.partial(kernel, Z, S, Y, W, U),
+    return pl.pallas_call(
+        functools.partial(kernel, Z, S, Y, W, U, caps),
         out_shape=shapes,
-        in_specs=[pl.BlockSpec(memory_space=pltpu.SMEM), vmem, vmem] + [hbm] * 5,
+        in_specs=[smem] * 3 + [vmem] * 2 + [hbm] * 5,
         out_specs=[hbm] * 5,
         scratch_shapes=scratch,
         compiler_params=pltpu.CompilerParams(
-            collective_id=0, has_side_effects=True, vmem_limit_bytes=63 * 1024 * 1024),
+            collective_id=level, has_side_effects=True, vmem_limit_bytes=63 * 1024 * 1024),
         cost_estimate=pl.CostEstimate(flops=18 * CHUNKS * R * W * U, bytes_accessed=10 * 2**20, transcendentals=0),
-    )(slot_group, column_group, row_mask, tokens.reshape(group_len, W), cotangent.reshape(group_len, W),
-      w_up, w_gate, w_down)
+    )(slots, sums, sort_orders, column_group, row_mask, tokens, cotangent, w_up, w_gate, w_down)
+
+
+def hand_over(*refs):
+    n = len(refs) // 2
+    sems = refs[-1]
+    copies = [pltpu.make_async_copy(refs[i], refs[n + i], sems.at[i]) for i in range(n)]
+    for copy in copies:
+        copy.start()
+    for copy in copies:
+        copy.wait()
+
+
+def body(tokens, cotangent, block_masks, w_up, w_gate, w_down):
+    owners, Y = lax.axis_size("seq"), lax.axis_size("ffn")
+    S, Z = PLANE, owners // PLANE
+    _, group_len, W = tokens.shape
+    groups = block_masks.shape[0]
+    U = w_up.shape[1]
+    owner_blocks = U // BLK
+    quarter = S * CAP * ROWS // Y
+    hops = hop_counts(Z)
+    my_owner = lax.axis_index("seq")
+    z, s = my_owner // S, my_owner % S
+
+    live = block_masks > 0
+    need = jnp.any(live.reshape(Z, S, Z, S * owner_blocks), axis=3)
+    planes = jnp.arange(Z)
+    onward = (planes[None, :] - planes[:, None]) % Z
+    reach, rank, order = {}, {}, {}
+    group_in_plane = jnp.arange(S, dtype=jnp.int32)
+    for direction in range(2):
+        distance = onward if direction == 0 else (Z - onward) % Z
+        for limit in sorted(set(hops[0])):
+            usable = need & (distance <= limit)[:, None, :]
+            far = jnp.max(jnp.where(usable, distance[:, None, :], 0), axis=2)
+            key = far * S + (S - 1 - group_in_plane)
+            place = jnp.sum((key[:, None, :] > key[:, :, None]).astype(jnp.int32), axis=2)
+            reach[direction, limit], rank[direction, limit] = far, place
+            order[direction, limit] = jnp.sum(
+                jnp.where(place[:, None, :] == group_in_plane[None, :, None], group_in_plane[None, None, :], 0), axis=2)
+
+    mine = lax.dynamic_slice_in_dim(live, z * S * owner_blocks, S * owner_blocks, 1)
+    active = jnp.any(mine.reshape(groups, S, owner_blocks), axis=2).T
+    ordinal = jnp.cumsum(active.astype(jnp.int32), axis=1) - 1
+    slot_ids = jnp.arange(CAP, dtype=jnp.int32)
+    picked = (ordinal[:, None, :] == slot_ids[None, :, None]) & active[:, None, :]
+    group_ids = jnp.arange(groups, dtype=jnp.int32)
+    held = jnp.any(picked, axis=2).reshape(-1)
+    picked_rows = picked.reshape(S * CAP, groups)
+
+    def look_up(table):
+        return jnp.sum(jnp.where(picked_rows, table.reshape(1, groups), 0), axis=1)
+    slot_group = look_up(group_ids)
+    held_group = jnp.where(held, slot_group, -1)
+    away_of = jnp.where(held, (z - slot_group // S) % Z, 0)
+    slot_place, sum_orders, sort_orders = [], [], []
+    for a in range(2):
+        ranks = [look_up(rank[d, hops[a][d]]) for d in range(2)]
+        place = jnp.where(away_of <= hops[a][0], ranks[0], ranks[1])
+        place = jnp.where(away_of == 0, jnp.where(held, slot_group % S, 0), place)
+        slot_place.append((away_of, place))
+        sum_orders.append([])
+        for d in range(2):
+            sort_orders.append(lax.dynamic_index_in_dim(order[d, hops[a][d]], z, 0, keepdims=False))
+            row = []
+            for far in range(1, hops[a][d] + 1):
+                target = (z + far) % Z if d == 0 else (z + Z - far) % Z
+                row.append(target * S + lax.dynamic_index_in_dim(order[1 - d, hops[a][d]], target, 0, keepdims=False))
+            sum_orders[a].append(row)
+    sort_orders = jnp.stack(sort_orders)
+    own_groups = z * S + group_in_plane
+
+    my_picked = lax.dynamic_index_in_dim(picked, s, 0, keepdims=False)
+    my_columns = lax.dynamic_slice_in_dim(block_masks, my_owner * owner_blocks, owner_blocks, 1)
+    block_live = jnp.sum(jnp.where(my_picked[:, :, None], my_columns[None], 0), axis=1).astype(F32)
+    unit_live = jnp.repeat(block_live, BLK, axis=1)
+    row_mask = jnp.broadcast_to(
+        unit_live[None, :, None, :], (quarter // (CAP * ROWS), CAP, ROWS, U)).reshape(quarter, U)
+
+    table = levels(Z, S)
+    branches = [functools.partial(ffn, i, caps, Z, S, Y, U) for i, caps in enumerate(table)]
+    level = jnp.int32(0)
+    for caps in table[:-1]:
+        fits = jnp.bool_(True)
+        for (direction, limit), far in reach.items():
+            for hop in range(1, limit + 1):
+                most = jnp.max(jnp.sum((far >= hop).astype(jnp.int32), axis=1))
+                fits = fits & (most <= caps[limit][hop - 1])
+        level = level + jnp.where(fits, 0, 1)
+    arguments = (held_group, slot_place, (own_groups, sum_orders), sort_orders, row_mask,
+                 tokens.reshape(group_len, W), cotangent.reshape(group_len, W), w_up, w_gate, w_down)
+    results = branches[0](*arguments) if len(table) == 1 else lax.switch(level, branches, *arguments)
+    hbm = pl.BlockSpec(memory_space=pl.ANY)
+    results = pl.pallas_call(
+        hand_over, out_shape=tuple(jax.ShapeDtypeStruct(r.shape, r.dtype) for r in results),
+        in_specs=[hbm] * len(results), out_specs=[hbm] * len(results),
+        scratch_shapes=[pltpu.SemaphoreType.DMA((len(results),))])(*results)
+    outputs, grad_tokens, grad_up, grad_gate, grad_down = results
     return outputs[None], grad_tokens[None], grad_up, grad_gate, grad_down
 
 

time: 386 us -> 540 us (1.40)
  Pallas kernels: 373 us -> 502 us
  between operations: 0.73 us -> 18.2 us
  other arithmetic: 0.87 us -> 15.5 us
  local copies, waits for them, and re-layouts: 11.3 us -> 3.42 us
    pallas_call x1 -> x2, Pallas kernels: 373 us -> 502 us  [the longest x1 342 us: ffn(): pl.pallas_call(functools.partial(kernel, Z, S, Y, W, U, caps), out_shape=...]
    reduce_max x1 -> x15, other arithmetic: 0.04 us -> 9.52 us  [the longest x14 8.89 us: body(): most = jnp.max(jnp.sum((far >= hop).astype(jnp.int32), axis=1))]
    unnamed x20 -> x4, local copies, waits for them, and re-layouts: 9.56 us -> 0.73 us
where the time goes in v2:
time: 540 us
  Pallas kernels  502 us (93%)
  between operations  18.2 us (3%)
  other arithmetic  15.5 us (3%)
    pallas_call x1, Pallas kernels, ffn(): pl.pallas_call(functools.partial(kernel, Z, S, Y, W, U, caps), out_shape=...  342 us
    pallas_call x1, Pallas kernels, body(): pl.pallas_call(hand_over, out_shape=tuple((jax.ShapeDtypeStruct(r.shape,...  160 us

profile of v2, /device:TPU:1, one launch (start us, length us, event | category | flops | bytes accessed | tf_op | source)
XLA Modules:
  0.0 539.9 jit_solution(15291871893624840052)
XLA Ops:
  0.9 0.7 copy-done
  1.6 0.1 constant_dynamic-slice_fusion.20
  1.8 0.2 reduce_window_sum.11
  2.2 0.2 reshape.362
  2.4 1.2 reduce_or.27
  3.5 0.6 select_reduce_fusion.10
  4.2 0.1 convert_reduce_fusion.4
  4.3 0.6 reduce_max.182
  6.2 0.6 reduce_max.183
  8.2 0.6 reduce_max.184
  10.1 0.6 reduce_max.188
  12.0 0.3 convert_reduce_fusion
  12.3 0.1 broadcast_in_dim.268
  12.4 0.2 select_reduce_fusion.9
  12.7 0.1 convert_reduce_fusion.8
  12.8 0.6 reduce_max.175
  14.7 0.6 reduce_max.176
  16.7 0.6 reduce_max.177
  18.0 0.3 convert_reduce_fusion.2
  18.2 0.1 broadcast_in_dim.264
  18.3 0.2 select_reduce_fusion.7
  18.6 0.1 convert_reduce_fusion.15
  18.7 0.6 reduce_max.160
  20.7 0.6 reduce_max.161
  22.6 0.6 reduce_max.162
  23.9 0.1 convert_reduce_fusion.11
  24.0 0.6 reduce_max.167
  26.0 0.6 reduce_max.168
  27.9 0.6 reduce_max.169
  29.9 0.6 reduce_max.170
  31.9 0.3 convert_reduce_fusion.3
  32.2 0.1 broadcast_in_dim.262
  32.2 0.2 select_reduce_fusion.6
  32.5 0.3 convert_reduce_fusion.1
  32.8 0.1 broadcast_in_dim.266
  32.9 0.2 select_reduce_fusion.8
  33.1 0.8 select_reduce_fusion.14
  34.2 0.1 reduce_sum.387
  34.3 0.2 select_reduce_fusion.19
  34.5 0.2 reduce_or.29
  34.8 0.1 reshape.364
  34.9 344.8 %conditional.1 = ((bf16[256,2048]{1,0:T(8,128)(2,1)}, bf16[256,2048]{1,0:T(8,128)(2,1)}, bf16[2048,256]{1,0:T(8,128)(2,1)}, bf16[2048,256]{1,0:T(8,128)(2,1)}, bf16[256,2048]{1,0:T(8,128)(2,1)})) conditional(s32[]{:T(128)} %clamp.3, (s32[24]{0:T(128)S(1)}, s32[24]{0:T(128)S(1)}, s32[24]{0:T(128)S(1)}, ...), branch_computations={%region_50.53_spmd.clone, %region_53.56_spmd.clone, %region_56.59_... | conditional | flops 7247758336 | bytes 10493056 | solution.py:645
  35.4 0.6 concatenate.10.sums
  36.1 0.1 select_reduce_fusion.3
  36.2 0.6 pad_add_fusion.1.slots
  36.8 0.6 reshape.369.column_group
  37.5 341.7 %branch_1_fun.1 = (bf16[256,2048]{1,0:T(8,128)(2,1)}, bf16[256,2048]{1,0:T(8,128)(2,1)}, bf16[2048,256]{1,0:T(8,128)(2,1)}, bf16[2048,256]{1,0:T(8,128)(2,1)}, bf16[256,2048]{1,0:T(8,128)(2,1)}) custom-call(s32[2,24]{1,0:T(2,128)} %pad_add_fusion.1.slots, s32[92]{0:T(128)} %concatenate.10.sums, s32[4,8]{1,0:T(4,128)S(1)} %get-tuple-element.359.orders, ...), custom_call_target="tpu_custom_call" | custom-call | flops 7247757312 | bytes 10485760 | tf_op jit(solution)/shard_map/cond/branch_1_fun/pallas_call | solution.py:544
  379.7 160.0 %shard_map.167 = (bf16[256,2048]{1,0:T(8,128)(2,1)}, bf16[256,2048]{1,0:T(8,128)(2,1)}, bf16[2048,256]{1,0:T(8,128)(2,1)}, bf16[2048,256]{1,0:T(8,128)(2,1)}, bf16[256,2048]{1,0:T(8,128)(2,1)}) custom-call(bf16[256,2048]{1,0:T(8,128)(2,1)} %get-tuple-element.267.refs_0_, bf16[256,2048]{1,0:T(8,128)(2,1)} %get-tuple-element.268.refs_1_, ...), custom_call_target="tpu_custom_call" | custom-call | tf_op jit(solution)/shard_map/pallas_call | solution.py:647
  (36 shorter events, 1.0 us)
Async XLA Ops:
  0.8 0.8 copy-start
  35.4 0.7 copy-start.1
  35.4 0.7 copy-start.5

commit v3 on v2

--- a/solution.py
+++ b/solution.py
@@ -95,39 +95,44 @@
     def arrivals(a, direction, hop, count):
         return pl.ds(blocks[a][direction][hop - 1], count)
 
-    def ag_copy(u, direction, hop):
-        a = u % 2
+    def ag_copy(u, half, direction, hop):
+        a, columns = u % 2, half_of(half)
         count = caps[hops[a][direction]][hop - 1]
-        source = sorted_rows[a][direction] if hop == 1 else ag[u].at[arrivals(a, direction, hop - 1, count)]
+        if hop == 1:
+            source = sorted_rows[a][direction].at[:, :, columns]
+        else:
+            source = ag[u].at[arrivals(a, direction, hop - 1, count), :, columns]
         return pltpu.make_async_remote_copy(
-            src_ref=source, dst_ref=ag[u].at[arrivals(a, direction, hop, count)],
-            send_sem=ag_send.at[u, direction, hop - 1], recv_sem=ag_recv.at[u, direction, hop - 1],
+            src_ref=source, dst_ref=ag[u].at[arrivals(a, direction, hop, count), :, columns],
+            send_sem=ag_send.at[u, half, direction, hop - 1], recv_sem=ag_recv.at[u, half, direction, hop - 1],
             device_id=along_z(direction), device_id_type=MESH)
 
     def ag_start(u):
         a = u % 2
         settle(ag[u].at[pl.ds(0, S)], sp_recv.at[u])
-        for direction in range(2):
-            target = sorted_rows[a][direction]
-            if u >= 2:
-                ag_copy(u - 2, direction, 1).wait_send()
-
-            def step(columns):
-                own = ag[u][0:S, :, columns].reshape(S * ROWS, columns.size)
-                moved = dot(sort[a][direction][...], own, (1, 0)).astype(BF16)
-                target[:, :, columns] = moved.reshape(target.shape[0], ROWS, columns.size)
-            feature_loop(min(512, W), step)
-            ag_copy(u, direction, 1).start()
-
-    def ag_forward(u, hop):
+        for half in range(2):
+            for direction in range(2):
+                target = sorted_rows[a][direction]
+                if u >= 2:
+                    ag_copy(u - 2, half, direction, 1).wait_send()
+
+                def step(columns):
+                    own = ag[u][0:S, :, columns].reshape(S * ROWS, columns.size)
+                    moved = dot(sort[a][direction][...], own, (1, 0)).astype(BF16)
+                    target[:, :, columns] = moved.reshape(target.shape[0], ROWS, columns.size)
+                half_loop(half, step)
+                ag_copy(u, half, direction, 1).start()
+
+    def ag_forward(u, hop, half):
         for direction in range(2):
             if hop <= hops[u % 2][direction]:
-                ag_copy(u, direction, hop - 1).wait_recv()
-                ag_copy(u, direction, hop).start()
+                ag_copy(u, half, direction, hop - 1).wait_recv()
+                ag_copy(u, half, direction, hop).start()
 
     def ag_finish(u):
-        for direction in range(2):
-            ag_copy(u, direction, hops[u % 2][direction]).wait_recv()
+        for half in range(2):
+            for direction in range(2):
+                ag_copy(u, half, direction, hops[u % 2][direction]).wait_recv()
 
     def pack(u):
         a = u % 2
@@ -152,6 +157,18 @@
             fn(pl.ds(pl.multiple_of(b * width, width), width))
             return carry
         lax.fori_loop(0, W // width, step, 0)
+
+    HALF = W // 2
+    piece_width = min(512, HALF)
+
+    def half_of(half):
+        return pl.ds(half * HALF, HALF)
+
+    def half_loop(half, fn):
+        def step(b, carry):
+            fn(pl.ds(pl.multiple_of(half * HALF + b * piece_width, piece_width), piece_width))
+            return carry
+        lax.fori_loop(0, HALF // piece_width, step, 0)
 
     def wide(ref, columns):
         return ref[:, :, :, columns].reshape(R, columns.size)
@@ -272,21 +289,25 @@
     def received(a, direction, hop, count):
         return rs[a].at[pl.ds(room[a][direction][hop - 1], count)]
 
-    def rs_copy(u, direction, hop):
-        a = u % 2
+    def rs_copy(u, half, direction, hop):
+        a, columns = u % 2, half_of(half)
         counts = caps[hops[a][direction]]
         count = counts[len(counts) - hop]
-        source = first[a][direction] if hop == 1 else received(a, direction, hop - 1, count)
+        if hop == 1:
+            source = first[a][direction].at[:, :, columns]
+        else:
+            source = received(a, direction, hop - 1, count).at[:, :, columns]
         return pltpu.make_async_remote_copy(
-            src_ref=source, dst_ref=received(a, direction, hop, count),
-            send_sem=rs_send.at[u, direction, hop - 1], recv_sem=rs_recv.at[u, direction, hop - 1],
+            src_ref=source, dst_ref=received(a, direction, hop, count).at[:, :, columns],
+            send_sem=rs_send.at[u, half, direction, hop - 1], recv_sem=rs_recv.at[u, half, direction, hop - 1],
             device_id=along_z(direction), device_id_type=MESH)
 
-    def release(u, direction):
+    def release(u, half, direction):
         if u < 2:
-            pl.semaphore_signal(free.at[u, direction], inc=1, device_id=along_z(1 - direction), device_id_type=MESH)
-
-    def rs_step(u, direction, hop):
+            pl.semaphore_signal(
+                free.at[u, half, direction], inc=1, device_id=along_z(1 - direction), device_id_type=MESH)
+
+    def rs_step(u, half, direction, hop):
         a = u % 2
         last = hops[a][direction]
         if hop > last:
@@ -294,15 +315,15 @@
         far = last - hop + 1
         if hop == 1:
             if u >= 2:
-                rs_copy(u - 2, direction, 1).wait_send()
+                rs_copy(u - 2, half, direction, 1).wait_send()
 
             def step(columns):
                 first[a][direction][:, :, columns] = plane_sum(u, direction, far, columns).astype(BF16)
         else:
             if hop > 2:
-                rs_copy(u, direction, hop - 1).wait_send()
-                release(u, direction)
-            rs_copy(u, direction, hop - 1).wait_recv()
+                rs_copy(u, half, direction, hop - 1).wait_send()
+                release(u, half, direction)
+            rs_copy(u, half, direction, hop - 1).wait_recv()
             old = caps[last][far]
             arrived = received(a, direction, hop - 1, old)
             fresh = rs[a].at[pl.ds(room[a][direction][hop - 2] + old, caps[last][far - 1] - old)]
@@ -312,35 +333,42 @@
                 arrived[:, :, columns] = (arrived[:, :, columns].astype(F32) + total[:old]).astype(BF16)
                 if caps[last][far - 1] > old:
                     fresh[:, :, columns] = total[old:].astype(BF16)
-        feature_loop(min(512, W), step)
+        half_loop(half, step)
         if u >= 2:
-            pl.semaphore_wait(free.at[u - 2, direction], 1)
-        rs_copy(u, direction, hop).start()
-
-    def rs_both(u, hop):
+            pl.semaphore_wait(free.at[u - 2, half, direction], 1)
+        rs_copy(u, half, direction, hop).start()
+
+    def rs_both(u, hop, half):
         for direction in range(2):
-            rs_step(u, direction, hop)
+            rs_step(u, half, direction, hop)
+
+    def rs_start(u):
+        collected(u)
+        for half in range(2):
+            rs_both(u, 1, half)
 
     def finish(u):
         a, k = u % 2, u // 2
-        ends = []
-        for direction in range(2):
-            last = hops[a][direction]
-            if last > 1:
-                rs_copy(u, direction, last).wait_send()
-                release(u, direction)
-            rs_copy(u, direction, last).wait_recv()
-            ends.append(received(a, direction, last, caps[last][0]))
-
-        def step(columns):
-            total = plane_sum(u, 0, 0, columns)
+        for half in range(2):
+            ends = []
             for direction in range(2):
-                arrived = ends[direction][:, :, columns].reshape(-1, columns.size)
-                total = total + dot(sort[1 - a][1 - direction][...], arrived, (0, 0)).reshape(S, ROWS, columns.size)
-            fin[u][:, :, columns] = total.astype(BF16)
-        feature_loop(min(512, W), step)
-        for direction in range(2):
-            release(u, direction)
+                last = hops[a][direction]
+                if last > 1:
+                    rs_copy(u, half, direction, last).wait_send()
+                    release(u, half, direction)
+                rs_copy(u, half, direction, last).wait_recv()
+                ends.append(received(a, direction, last, caps[last][0]))
+
+            def step(columns):
+                total = plane_sum(u, 0, 0, columns)
+                for direction in range(2):
+                    arrived = ends[direction][:, :, columns].reshape(-1, columns.size)
+                    total = total + dot(sort[1 - a][1 - direction][...], arrived, (0, 0)).reshape(
+                        S, ROWS, columns.size)
+                fin[u][:, :, columns] = total.astype(BF16)
+            half_loop(half, step)
+            for direction in range(2):
+                release(u, half, direction)
         place = results[a].at[pl.ds(pl.multiple_of(s * SLICE + k * ROWS, ROWS), ROWS)]
 
         def go(t):
@@ -389,8 +417,7 @@
         greet(across_y(d))
     pl.semaphore_wait(barrier, S - 1 + 2 + Y - 1)
 
-    for u in range(4):
-        spread(u)
+    spread(0)
     for a in range(2):
         for direction in range(2):
             for r in range(caps[hops[a][direction]][0]):
@@ -399,7 +426,7 @@
                 hit = column == orders[2 * a + direction, r] * ROWS + row
                 sort[a][direction][r * ROWS:(r + 1) * ROWS, :] = jnp.where(hit, 1.0, 0.0).astype(BF16)
     ag_start(0)
-    ag_start(1)
+    spread(1)
 
     def select_rows(g, carry):
         row = lax.broadcasted_iota(jnp.int32, (ROWS, R), 0)
@@ -412,61 +439,72 @@
         copy.wait()
 
     far = max(hops[0])
-    for hop in range(2, far + 1):
-        ag_forward(0, hop)
-        ag_forward(1, hop)
-    ag_start(2)
-    ag_start(3)
-
-    def chunk_steps(k):
-        t, c = 2 * k, 2 * k + 1
-        return [
-            lambda: (ag_finish(t), pack(t), ag_finish(c), pack(c)),
-            lambda: (rows_ready(t), up_and_gate(k)),
-            lambda: (rows_ready(c), hidden_grad(k), sum_send(k)),
-            lambda: activate(k),
-            lambda: (act_ready(k), down(k)),
-            lambda: back(k),
-        ]
-
-    def weave(main, beside):
-        n = max(len(main), len(beside))
-        for i in range(n):
-            if i < len(main):
-                main[i]()
-            if i < len(beside):
-                beside[i]()
-
-    weave(chunk_steps(0), [functools.partial(ag_forward, u, hop) for hop in range(2, far + 1) for u in (2, 3)])
-    for u in (0, 1):
-        collected(u)
-        rs_both(u, 1)
-    weave(chunk_steps(1), [functools.partial(rs_both, u, hop) for hop in range(2, far + 1) for u in (0, 1)])
-    finish(0)
-    finish(1)
-    for u in (2, 3):
-        collected(u)
-        rs_both(u, 1)
-    weave([functools.partial(token_weight_grad, 1, wu, gu_out), functools.partial(token_weight_grad, 2, wg, gg_out),
-           functools.partial(down_weight_grad, wd, gd_out)],
-          [functools.partial(rs_both, u, hop) for hop in range(2, far + 1) for u in (2, 3)])
-    finish(2)
+
+    def run(step, u, pieces):
+        events = [(hop, half) for hop in range(2, far + 1) for half in range(2)]
+        for fn in pieces.get(0, ()):
+            fn()
+        for i, (hop, half) in enumerate(events):
+            step(u, hop, half)
+            for fn in pieces.get(i + 1, ()):
+                fn()
+        for i in range(len(events) + 1, 8):
+            for fn in pieces.get(i, ()):
+                fn()
+
+    def each(*fns):
+        return tuple(functools.partial(*fn) for fn in fns)
+
+    run(ag_forward, 0, {2: each((ag_start, 1), (spread, 2))})
+    run(ag_forward, 1, {
+        0: each((ag_finish, 0), (pack, 0)),
+        2: each((ag_start, 2), (spread, 3)),
+        5: each((rows_ready, 0), (up_and_gate, 0))})
+    run(ag_forward, 2, {
+        0: each((ag_finish, 1), (pack, 1)),
+        2: each((ag_start, 3)),
+        5: each((rows_ready, 1), (hidden_grad, 0), (sum_send, 0))})
+    run(ag_forward, 3, {
+        0: each((ag_finish, 2), (pack, 2)),
+        1: each((activate, 0)),
+        3: each((act_ready, 0), (down, 0)),
+        6: each((rows_ready, 2), (up_and_gate, 1), (ag_finish, 3), (pack, 3))})
+    rs_start(0)
+    run(rs_both, 0, {
+        0: each((back, 0)),
+        5: each((rows_ready, 3), (hidden_grad, 1), (sum_send, 1)),
+        6: each((rs_start, 1), (activate, 1))})
+    run(rs_both, 1, {
+        0: each((finish, 0)),
+        1: each((act_ready, 1), (down, 1)),
+        4: each((back, 1)),
+        6: each((rs_start, 2))})
+    run(rs_both, 2, {
+        0: each((finish, 1)),
+        2: each((token_weight_grad, 1, wu, gu_out)),
+        4: each((token_weight_grad, 2, wg, gg_out)),
+        6: each((rs_start, 3))})
+    run(rs_both, 3, {
+        0: each((finish, 2)),
+        2: each((down_weight_grad, wd, gd_out))})
     finish(3)
 
     for u in range(4):
         a, k = u % 2, u // 2
         settle(sources[a].at[pl.ds(0, (S - 1) * ROWS)], sp_send.at[u])
-        for direction in range(2):
-            for hop in range(1 if k else 2, hops[a][direction] + 1):
-                ag_copy(u, direction, hop).wait_send()
+        for half in range(2):
+            for direction in range(2):
+                for hop in range(1 if k else 2, hops[a][direction] + 1):
+                    ag_copy(u, half, direction, hop).wait_send()
         settle(fin[u].at[pl.ds(0, S - 1)], fin_send.at[u])
         settle(results[a].at[pl.ds(0, S * ROWS)], out_recv.at[u])
     for u in (2, 3):
         a = u % 2
         settle(pk[a].at[pl.ds(0, S - 1)], pk_send.at[u])
         settle(op[a].at[pl.ds(0, S - 1)], op_send.at[u])
-        for direction in range(2):
-            rs_copy(u, direction, 1).wait_send()
+        for half in range(2):
+            for direction in range(2):
+                rs_copy(u, half, direction, 1).wait_send()
     settle(part.at[pl.ds(0, Y - 1)], y_send.at[1, 0])
     for k in range(CHUNKS):
         settle(act[k].at[pl.ds(0, Y - 1)], y_send.at[k, 1])
@@ -532,9 +570,9 @@
         + [pltpu.VMEM((sums.shape[0] * ROWS, R), BF16)]
         + [pltpu.VMEM((counts(a, d)[0] * ROWS, S * ROWS), BF16) for a, d in ways]
         + [
-            dma((3,)), dma((4,)), dma((4,)), dma((4, 2, half)), dma((4, 2, half)), dma((4,)), dma((4,)),
-            dma((2, 2)), dma((2, 2)), dma((4,)), dma((4,)), dma((4, 2, half)), dma((4, 2, half)), dma((4,)),
-            dma((4,)), dma((3,)), pltpu.SemaphoreType.REGULAR((2, 2)),
+            dma((3,)), dma((4,)), dma((4,)), dma((4, 2, 2, half)), dma((4, 2, 2, half)), dma((4,)), dma((4,)),
+            dma((2, 2)), dma((2, 2)), dma((4,)), dma((4,)), dma((4, 2, 2, half)), dma((4, 2, 2, half)), dma((4,)),
+            dma((4,)), dma((3,)), pltpu.SemaphoreType.REGULAR((2, 2, 2)),
         ]
     )
     shapes = (
@@ -555,12 +593,8 @@
 
 def hand_over(*refs):
     n = len(refs) // 2
-    sems = refs[-1]
-    copies = [pltpu.make_async_copy(refs[i], refs[n + i], sems.at[i]) for i in range(n)]
-    for copy in copies:
-        copy.start()
-    for copy in copies:
-        copy.wait()
+    for i in range(n):
+        refs[n + i][...] = refs[i][...]
 
 
 def body(tokens, cotangent, block_masks, w_up, w_gate, w_down):
@@ -579,18 +613,17 @@
     need = jnp.any(live.reshape(Z, S, Z, S * owner_blocks), axis=3)
     planes = jnp.arange(Z)
     onward = (planes[None, :] - planes[:, None]) % Z
-    reach, rank, order = {}, {}, {}
     group_in_plane = jnp.arange(S, dtype=jnp.int32)
-    for direction in range(2):
-        distance = onward if direction == 0 else (Z - onward) % Z
-        for limit in sorted(set(hops[0])):
-            usable = need & (distance <= limit)[:, None, :]
-            far = jnp.max(jnp.where(usable, distance[:, None, :], 0), axis=2)
-            key = far * S + (S - 1 - group_in_plane)
-            place = jnp.sum((key[:, None, :] > key[:, :, None]).astype(jnp.int32), axis=2)
-            reach[direction, limit], rank[direction, limit] = far, place
-            order[direction, limit] = jnp.sum(
-                jnp.where(place[:, None, :] == group_in_plane[None, :, None], group_in_plane[None, None, :], 0), axis=2)
+    limits = sorted(set(hops[0]))
+    keys = [(direction, limit) for direction in range(2) for limit in limits]
+    distance = jnp.stack([onward if direction == 0 else (Z - onward) % Z for direction, _ in keys])
+    limit_of = jnp.asarray([limit for _, limit in keys])[:, None, None]
+    distance = jnp.where(distance <= limit_of, distance, 0).astype(jnp.int32)
+    reach = jnp.max(jnp.where(need[None], distance[:, :, None, :], 0), axis=3)
+    key = reach * S + (S - 1 - group_in_plane)
+    rank = jnp.sum((key[:, :, None, :] > key[:, :, :, None]).astype(jnp.int32), axis=3)
+    order = jnp.sum(
+        jnp.where(rank[:, :, None, :] == group_in_plane[:, None], group_in_plane, 0), axis=3)
 
     mine = lax.dynamic_slice_in_dim(live, z * S * owner_blocks, S * owner_blocks, 1)
     active = jnp.any(mine.reshape(groups, S, owner_blocks), axis=2).T
@@ -608,17 +641,17 @@
     away_of = jnp.where(held, (z - slot_group // S) % Z, 0)
     slot_place, sum_orders, sort_orders = [], [], []
     for a in range(2):
-        ranks = [look_up(rank[d, hops[a][d]]) for d in range(2)]
+        ranks = [look_up(rank[keys.index((d, hops[a][d]))]) for d in range(2)]
         place = jnp.where(away_of <= hops[a][0], ranks[0], ranks[1])
         place = jnp.where(away_of == 0, jnp.where(held, slot_group % S, 0), place)
         slot_place.append((away_of, place))
         sum_orders.append([])
         for d in range(2):
-            sort_orders.append(lax.dynamic_index_in_dim(order[d, hops[a][d]], z, 0, keepdims=False))
+            sort_orders.append(lax.dynamic_index_in_dim(order[keys.index((d, hops[a][d]))], z, 0, keepdims=False))
             row = []
             for far in range(1, hops[a][d] + 1):
                 target = (z + far) % Z if d == 0 else (z + Z - far) % Z
-                row.append(target * S + lax.dynamic_index_in_dim(order[1 - d, hops[a][d]], target, 0, keepdims=False))
+                row.append(target * S + lax.dynamic_index_in_dim(order[keys.index((1 - d, hops[a][d]))], target, 0, keepdims=False))
             sum_orders[a].append(row)
     sort_orders = jnp.stack(sort_orders)
     own_groups = z * S + group_in_plane
@@ -632,22 +665,20 @@
 
     table = levels(Z, S)
     branches = [functools.partial(ffn, i, caps, Z, S, Y, U) for i, caps in enumerate(table)]
-    level = jnp.int32(0)
-    for caps in table[:-1]:
-        fits = jnp.bool_(True)
-        for (direction, limit), far in reach.items():
-            for hop in range(1, limit + 1):
-                most = jnp.max(jnp.sum((far >= hop).astype(jnp.int32), axis=1))
-                fits = fits & (most <= caps[limit][hop - 1])
-        level = level + jnp.where(fits, 0, 1)
+    far = max(limits)
+    steps = jnp.arange(1, far + 1)[None, None, :, None]
+    most = jnp.max(jnp.sum((reach[:, :, None, :] >= steps).astype(jnp.int32), axis=3), axis=1)
+    allowed = [[list(caps[limit]) + [0] * (far - limit) for _, limit in keys] for caps in table]
+    level = jnp.sum(jnp.any(most[None] > jnp.asarray(allowed[:-1], jnp.int32).reshape(-1, len(keys), far),
+                            axis=(1, 2)).astype(jnp.int32))
     arguments = (held_group, slot_place, (own_groups, sum_orders), sort_orders, row_mask,
                  tokens.reshape(group_len, W), cotangent.reshape(group_len, W), w_up, w_gate, w_down)
     results = branches[0](*arguments) if len(table) == 1 else lax.switch(level, branches, *arguments)
-    hbm = pl.BlockSpec(memory_space=pl.ANY)
+    parts = 8
+    specs = [pl.BlockSpec((r.shape[0] // parts, r.shape[1]), lambda i: (i, 0)) for r in results]
     results = pl.pallas_call(
-        hand_over, out_shape=tuple(jax.ShapeDtypeStruct(r.shape, r.dtype) for r in results),
-        in_specs=[hbm] * len(results), out_specs=[hbm] * len(results),
-        scratch_shapes=[pltpu.SemaphoreType.DMA((len(results),))])(*results)
+        hand_over, out_shape=tuple(jax.ShapeDtypeStruct(r.shape, r.dtype) for r in results), grid=(parts,),
+        in_specs=specs, out_specs=specs)(*results)
     outputs, grad_tokens, grad_up, grad_gate, grad_down = results
     return outputs[None], grad_tokens[None], grad_up, grad_gate, grad_down
 

time: 540 us -> 315 us (0.58)
  Pallas kernels: 502 us -> 301 us
  between operations: 18.2 us -> 1.8 us
  other arithmetic: 15.5 us -> 6.72 us
    pallas_call x1, Pallas kernels: 160 us -> 7.25 us  [body(): pl.pallas_call(hand_over, out_shape=tuple((jax.ShapeDtypeStruct(r.shape,...]
    pallas_call x1, Pallas kernels: 342 us -> 294 us  [ffn(): pl.pallas_call(functools.partial(kernel, Z, S, Y, W, U, caps), out_shape=...]
    reduce_max x15 -> x2, other arithmetic: 9.52 us -> 0.77 us  [the longest x1 0.62 us: body(): reach = jnp.max(jnp.where(need[None], distance[:, :, None, :], 0), axis=3)]
where the time goes in v3:
time: 315 us
  Pallas kernels  301 us (96%)
  other arithmetic  6.72 us (2%)
  local copies, waits for them, and re-layouts  4.63 us (1%)
    pallas_call x1, Pallas kernels, ffn(): pl.pallas_call(functools.partial(kernel, Z, S, Y, W, U, caps), out_shape=...  294 us
    pallas_call x1, Pallas kernels, body(): pl.pallas_call(hand_over, out_shape=tuple((jax.ShapeDtypeStruct(r.shape,...  7.25 us

profile of v3, /device:TPU:1, one launch (start us, length us, event | category | flops | bytes accessed | tf_op | source)
XLA Modules:
  0.0 315.1 jit_solution(4875555971982938765)
XLA Ops:
  0.8 0.0 copy-start
  0.9 0.7 copy-done
  1.6 0.1 constant_dynamic-slice_fusion.20
  1.6 0.1 copy.40
  1.8 0.2 reduce_window_sum.11
  2.0 0.0 copy-start.2
  2.0 0.6 copy-done.2
  2.7 0.1 compare_select_fusion
  2.8 0.1 constant_dynamic-slice_fusion
  2.8 0.1 copy.53
  2.9 0.2 reshape.335
  3.1 1.2 reduce_or.36
  4.2 0.6 select_reduce_fusion.7
  4.9 0.4 convert_reduce_fusion.1
  5.3 0.0 copy-start.1
  5.3 0.1 reduce_max.19
  5.5 0.5 copy-done.1
  6.0 0.1 compare_reduce_fusion
  6.1 0.6 convert_reduce_fusion.2
  7.4 0.7 convert_reduce_fusion
  8.1 0.6 select_reduce_fusion.6
  8.7 0.1 broadcast_in_dim.213
  8.9 0.1 broadcast_in_dim.219
  9.0 0.1 broadcast_in_dim.217
  9.1 0.1 broadcast_in_dim.215
  9.2 0.8 select_reduce_fusion.8
  10.0 0.1 reduce_sum.166
  10.0 0.1 reduce_sum.164
  10.1 0.1 reduce_sum.162
  10.2 0.1 reduce_sum.160
  10.3 0.1 reduce_sum.157
  10.4 0.2 select_reduce_fusion.13
  10.5 0.1 broadcast_bitcast_fusion
  10.6 0.2 reduce_or.39
  10.8 0.1 reshape.337
  11.0 296.7 %conditional.1 = ((bf16[256,2048]{1,0:T(8,128)(2,1)}, bf16[256,2048]{1,0:T(8,128)(2,1)}, bf16[2048,256]{1,0:T(8,128)(2,1)}, bf16[2048,256]{1,0:T(8,128)(2,1)}, bf16[256,2048]{1,0:T(8,128)(2,1)})) conditional(s32[]{:T(128)} %clamp.3, (s32[24]{0:T(128)S(1)}, s32[24]{0:T(128)S(1)}, s32[24]{0:T(128)S(1)}, ...), branch_computations={%region_17.20_spmd.clone, %region_20.23_spmd.clone, %region_23.26_... | conditional | flops 7247758336 | bytes 10493056 | solution.py:676
  11.3 0.0 copy-start.5
  11.3 0.0 copy-start.6
  11.3 0.6 concatenate.16.sums
  11.9 0.0 copy-done.5
  11.9 0.0 copy-done.6
  12.0 0.1 select_reduce_fusion.1
  12.0 0.6 pad_add_fusion.slots
  12.6 0.1 broadcast_in_dim.234
  12.7 0.6 reshape.341.column_group
  13.3 294.1 %branch_0_fun.1 = (bf16[256,2048]{1,0:T(8,128)(2,1)}, bf16[256,2048]{1,0:T(8,128)(2,1)}, bf16[2048,256]{1,0:T(8,128)(2,1)}, bf16[2048,256]{1,0:T(8,128)(2,1)}, bf16[256,2048]{1,0:T(8,128)(2,1)}) custom-call(s32[2,24]{1,0:T(2,128)} %pad_add_fusion.slots, s32[80]{0:T(128)} %concatenate.16.sums, s32[4,8]{1,0:T(4,128)S(1)} %get-tuple-element.307.orders, ...), custom_call_target="tpu_custom_call" | custom-call | flops 7247757312 | bytes 10485760 | tf_op jit(solution)/shard_map/cond/branch_0_fun/pallas_call | solution.py:582
  307.7 7.2 %shard_map.185 = (bf16[256,2048]{1,0:T(8,128)(2,1)}, bf16[256,2048]{1,0:T(8,128)(2,1)}, bf16[2048,256]{1,0:T(8,128)(2,1)}, bf16[2048,256]{1,0:T(8,128)(2,1)}, bf16[256,2048]{1,0:T(8,128)(2,1)}) custom-call(bf16[256,2048]{1,0:T(8,128)(2,1)} %get-tuple-element.267.refs_0_, bf16[256,2048]{1,0:T(8,128)(2,1)} %get-tuple-element.268.refs_1_, ...), custom_call_target="tpu_custom_call" | custom-call | tf_op jit(solution)/shard_map/pallas_call | solution.py:679
  (24 shorter events, 0.3 us)
Async XLA Ops:
  0.8 0.8 copy-start
  2.0 0.7 copy-start.2
  5.3 0.7 copy-start.1
  11.3 0.7 copy-start.5
  11.3 0.7 copy-start.6

commit v4 on v3

--- a/solution.py
+++ b/solution.py
@@ -38,16 +38,19 @@
 
 def kernel(Z, S, Y, W, U, caps, slots, sums, orders, column_group, row_mask, tok, cot, wu_in, wg_in, wd_in,
            out, gtok, gu_out, gg_out, gd_out,
-           ag0, ag1, ag2, ag3, so0, so1, so2, so3, pk0, pk1, rw0, rw1, rw2, rw3, wu, wg, wd, part, py0, py1, act0, act1,
-           op0, op1, pr0, pr1, pr2, pr3, rs0, rs1, f00, f01, f10, f11, fin0, fin1, fin2, fin3, sel,
-           sort0, sort1, sort2, sort3,
-           w_sem, sp_send, sp_recv, ag_send, ag_recv, pk_send, rw_recv, y_send, y_recv,
-           op_send, pr_recv, rs_send, rs_recv, fin_send, out_recv, g_sem, free):
-    ag, pk, rw = (ag0, ag1, ag2, ag3), (pk0, pk1), (rw0, rw1, rw2, rw3)
-    py, act = (py0, py1), (act0, act1)
-    op, pr = (op0, op1), (pr0, pr1, pr2, pr3)
-    rs, first, fin = (rs0, rs1), ((f00, f01), (f10, f11)), (fin0, fin1, fin2, fin3)
-    sorted_rows, sort = ((so0, so1), (so2, so3)), ((sort0, sort1), (sort2, sort3))
+           *refs):
+    refs = list(refs)
+
+    def take(*shape):
+        if not shape:
+            return refs.pop(0)
+        return [take(*shape[1:]) for _ in range(shape[0])]
+    ag, sorted_rows, pk, rw = take(4), take(2, 2, 2), take(2), take(4)
+    wu, wg, wd, part = take(4)
+    py, act, op, pr, rs, first, fin = take(2), take(2), take(2), take(4), take(2), take(2, 2, 2), take(4)
+    sel, sort = take(), take(2, 2)
+    (w_sem, sp_send, sp_recv, ag_send, ag_recv, pk_send, rw_recv, y_send, y_recv,
+     op_send, pr_recv, rs_send, rs_recv, fin_send, out_recv, g_sem, free) = take(17)
     sources, results = (tok, cot), (out, gtok)
     R = S * CAP * ROWS
     SLICE = CHUNKS * ROWS
@@ -56,7 +59,7 @@
     up_z, down_z = lax.rem(z + 1, Z), lax.rem(z + Z - 1, Z)
     toward = (up_z, down_z)
     hops = hop_counts(Z)
-    blocks = [offsets(caps, hops[a], S)[0] for a in range(2)]
+    blocks = [offsets(caps, hops[half], S)[0] for half in range(2)]
 
     def mate(d):
         return lax.rem(s + d, S)
@@ -76,8 +79,16 @@
             return carry
         lax.fori_loop(1, S, step, 0)
 
+    pending = {}
+
     def settle(ref, sem):
         pltpu.make_async_copy(ref, ref, sem).wait()
+
+    def expect(key, *wait):
+        pending[key] = functools.partial(*wait)
+
+    def await_(*key):
+        pending.pop(key)()
 
     def spread(u):
         source, k = sources[u % 2], u // 2
@@ -91,66 +102,80 @@
                 device_id=in_plane(t), device_id_type=MESH).start()
         each_mate(go)
         pltpu.make_async_copy(piece(s), ag[u].at[s], sp_recv.at[u]).start()
-
-    def arrivals(a, direction, hop, count):
-        return pl.ds(blocks[a][direction][hop - 1], count)
+        expect(("spread out", u), settle, source.at[pl.ds(0, (S - 1) * ROWS)], sp_send.at[u])
+        expect(("spread in", u), settle, ag[u].at[pl.ds(0, S)], sp_recv.at[u])
+
+    def arrivals(half, direction, hop, count):
+        return pl.ds(blocks[half][direction][hop - 1], count)
 
     def ag_copy(u, half, direction, hop):
-        a, columns = u % 2, half_of(half)
-        count = caps[hops[a][direction]][hop - 1]
+        columns = half_of(half)
+        count = caps[hops[half][direction]][hop - 1]
         if hop == 1:
-            source = sorted_rows[a][direction].at[:, :, columns]
+            source = sorted_rows[u % 2][half][direction]
         else:
-            source = ag[u].at[arrivals(a, direction, hop - 1, count), :, columns]
+            source = ag[u].at[arrivals(half, direction, hop - 1, count), :, columns]
         return pltpu.make_async_remote_copy(
-            src_ref=source, dst_ref=ag[u].at[arrivals(a, direction, hop, count), :, columns],
+            src_ref=source, dst_ref=ag[u].at[arrivals(half, direction, hop, count), :, columns],
             send_sem=ag_send.at[u, half, direction, hop - 1], recv_sem=ag_recv.at[u, half, direction, hop - 1],
             device_id=along_z(direction), device_id_type=MESH)
 
     def ag_start(u):
         a = u % 2
-        settle(ag[u].at[pl.ds(0, S)], sp_recv.at[u])
+        await_("spread in", u)
         for half in range(2):
             for direction in range(2):
-                target = sorted_rows[a][direction]
+                target = sorted_rows[a][half][direction]
                 if u >= 2:
-                    ag_copy(u - 2, half, direction, 1).wait_send()
-
-                def step(columns):
+                    await_("gather out", u - 2, half, direction, 1)
+
+                def step(columns, local):
                     own = ag[u][0:S, :, columns].reshape(S * ROWS, columns.size)
-                    moved = dot(sort[a][direction][...], own, (1, 0)).astype(BF16)
-                    target[:, :, columns] = moved.reshape(target.shape[0], ROWS, columns.size)
+                    moved = dot(sort[half][direction][...], own, (1, 0)).astype(BF16)
+                    target[:, :, local] = moved.reshape(target.shape[0], ROWS, columns.size)
                 half_loop(half, step)
-                ag_copy(u, half, direction, 1).start()
+                ag_send_on(u, half, direction, 1)
+
+    def ag_send_on(u, half, direction, hop):
+        copy = ag_copy(u, half, direction, hop)
+        copy.start()
+        expect(("gather out", u, half, direction, hop), copy.wait_send)
+        expect(("gather in", u, half, direction, hop), copy.wait_recv)
 
     def ag_forward(u, hop, half):
         for direction in range(2):
-            if hop <= hops[u % 2][direction]:
-                ag_copy(u, half, direction, hop - 1).wait_recv()
-                ag_copy(u, half, direction, hop).start()
+            if hop <= hops[half][direction]:
+                await_("gather in", u, half, direction, hop - 1)
+                ag_send_on(u, half, direction, hop)
 
     def ag_finish(u):
         for half in range(2):
             for direction in range(2):
-                ag_copy(u, half, direction, hops[u % 2][direction]).wait_recv()
+                await_("gather in", u, half, direction, hops[half][direction])
 
     def pack(u):
         a = u % 2
         if u >= 2:
-            settle(pk[a].at[pl.ds(0, S - 1)], pk_send.at[u - 2])
+            await_("rows out", u - 2)
 
         def go(t):
             for j in range(CAP):
-                pk[a][t, j] = ag[u][slots[a, t * CAP + j]]
+                for half in range(2):
+                    columns = half_of(half)
+                    pk[a][t, j, :, columns] = ag[u][slots[half, t * CAP + j], :, columns]
             pltpu.make_async_remote_copy(
                 src_ref=pk[a].at[t], dst_ref=rw[u].at[s], send_sem=pk_send.at[u], recv_sem=rw_recv.at[u],
                 device_id=in_plane(t), device_id_type=MESH).start()
         each_mate(go)
         for j in range(CAP):
-            rw[u][s, j] = ag[u][slots[a, s * CAP + j]]
+            for half in range(2):
+                columns = half_of(half)
+                rw[u][s, j, :, columns] = ag[u][slots[half, s * CAP + j], :, columns]
+        expect(("rows out", u), settle, pk[a].at[pl.ds(0, S - 1)], pk_send.at[u])
+        expect(("rows in", u), settle, rw[u].at[pl.ds(0, S - 1)], rw_recv.at[u])
 
     def rows_ready(u):
-        settle(rw[u].at[pl.ds(0, S - 1)], rw_recv.at[u])
+        await_("rows in", u)
 
     def feature_loop(width, fn):
         def step(b, carry):
@@ -166,7 +191,8 @@
 
     def half_loop(half, fn):
         def step(b, carry):
-            fn(pl.ds(pl.multiple_of(half * HALF + b * piece_width, piece_width), piece_width))
+            local = pl.multiple_of(b * piece_width, piece_width)
+            fn(pl.ds(pl.multiple_of(half * HALF + local, piece_width), piece_width), pl.ds(local, piece_width))
             return carry
         lax.fori_loop(0, HALF // piece_width, step, 0)
 
@@ -178,7 +204,7 @@
 
     def up_and_gate(k):
         if k:
-            settle(part.at[pl.ds(0, Y - 1)], y_send.at[k - 1, 0])
+            await_("sums out", k - 1)
         part[...] = jnp.zeros_like(part)
 
         def step(columns):
@@ -198,9 +224,11 @@
             pltpu.make_async_remote_copy(
                 src_ref=part.at[lax.rem(y + d, Y)], dst_ref=py[k].at[d - 1], send_sem=y_send.at[k, 0],
                 recv_sem=y_recv.at[k, 0], device_id=across_y(d), device_id_type=MESH).start()
+        expect(("sums out", k), settle, part.at[pl.ds(0, Y - 1)], y_send.at[k, 0])
+        expect(("sums in", k), settle, py[k], y_recv.at[k, 0])
 
     def activate(k):
-        settle(py[k], y_recv.at[k, 0])
+        await_("sums in", k)
         total = [part[y, i] for i in range(3)]
         for d in range(Y - 1):
             total = [total[i] + py[k][d, i] for i in range(3)]
@@ -215,9 +243,11 @@
             pltpu.make_async_remote_copy(
                 src_ref=act[k].at[y], dst_ref=act[k].at[y], send_sem=y_send.at[k, 1],
                 recv_sem=y_recv.at[k, 1], device_id=across_y(d), device_id_type=MESH).start()
+        expect(("act out", k), settle, act[k].at[pl.ds(0, Y - 1)], y_send.at[k, 1])
+        expect(("act in", k), settle, act[k].at[pl.ds(0, Y - 1)], y_recv.at[k, 1])
 
     def act_ready(k):
-        settle(act[k].at[pl.ds(0, Y - 1)], y_recv.at[k, 1])
+        await_("act in", k)
 
     def activation(k, i):
         return act[k][:, i].reshape(R, U)
@@ -231,11 +261,13 @@
                 device_id=in_plane(t), device_id_type=MESH).start()
         each_mate(go)
         pltpu.make_async_copy(op[a].at[s], pr[u].at[s], pr_recv.at[u]).start()
+        expect(("parts out", u), settle, op[a].at[pl.ds(0, S - 1)], op_send.at[u])
+        expect(("parts in", u), settle, pr[u], pr_recv.at[u])
 
     def down(k):
         u = 2 * k
         if k:
-            settle(op[0].at[pl.ds(0, S - 1)], op_send.at[u - 2])
+            await_("parts out", u - 2)
 
         def step(columns):
             product = dot(activation(k, 0), wd[:, columns], (1, 0))
@@ -246,7 +278,7 @@
     def back(k):
         u = 2 * k + 1
         if k:
-            settle(op[1].at[pl.ds(0, S - 1)], op_send.at[u - 2])
+            await_("parts out", u - 2)
 
         def step(columns):
             product = dot(activation(k, 1), wu[columns, :], (1, 1))
@@ -256,49 +288,48 @@
         give_back(u)
 
     def collected(u):
-        settle(pr[u], pr_recv.at[u])
+        await_("parts in", u)
 
     sum_rows = [S * ROWS]
     sum_at = []
-    for a in range(2):
+    for half in range(2):
         sum_at.append([])
         for direction in range(2):
             row = []
-            for count in caps[hops[a][direction]]:
+            for count in caps[hops[half][direction]]:
                 row.append(sum_rows[0])
                 sum_rows[0] += count * ROWS
-            sum_at[a].append(row)
-
-    def plane_sum(u, direction, far, columns):
-        a = u % 2
-        at, count = (0, S) if far == 0 else (sum_at[a][direction][far - 1], caps[hops[a][direction]][far - 1])
+            sum_at[half].append(row)
+
+    def plane_sum(u, half, direction, far, columns):
+        at, count = (0, S) if far == 0 else (sum_at[half][direction][far - 1], caps[hops[half][direction]][far - 1])
         pick = sel[at:at + count * ROWS, :]
         return dot(pick, wide(pr[u], columns), (1, 0)).reshape(count, ROWS, columns.size)
 
     room = []
-    for a in range(2):
+    for half in range(2):
         at, table = 0, []
         for direction in range(2):
-            row, counts = [], caps[hops[a][direction]]
+            row, counts = [], caps[hops[half][direction]]
             for hop in range(1, len(counts) + 1):
                 row.append(at)
                 at += counts[max(len(counts) - hop, 1) - 1]
             table.append(row)
         room.append(table)
 
-    def received(a, direction, hop, count):
-        return rs[a].at[pl.ds(room[a][direction][hop - 1], count)]
+    def received(a, half, direction, hop, count):
+        return rs[a].at[pl.ds(room[half][direction][hop - 1], count)]
 
     def rs_copy(u, half, direction, hop):
         a, columns = u % 2, half_of(half)
-        counts = caps[hops[a][direction]]
+        counts = caps[hops[half][direction]]
         count = counts[len(counts) - hop]
         if hop == 1:
-            source = first[a][direction].at[:, :, columns]
+            source = first[a][half][direction]
         else:
-            source = received(a, direction, hop - 1, count).at[:, :, columns]
+            source = received(a, half, direction, hop - 1, count).at[:, :, columns]
         return pltpu.make_async_remote_copy(
-            src_ref=source, dst_ref=received(a, direction, hop, count).at[:, :, columns],
+            src_ref=source, dst_ref=received(a, half, direction, hop, count).at[:, :, columns],
             send_sem=rs_send.at[u, half, direction, hop - 1], recv_sem=rs_recv.at[u, half, direction, hop - 1],
             device_id=along_z(direction), device_id_type=MESH)
 
@@ -306,37 +337,44 @@
         if u < 2:
             pl.semaphore_signal(
                 free.at[u, half, direction], inc=1, device_id=along_z(1 - direction), device_id_type=MESH)
+            n = sum(key[:4] == ("free", u, half, direction) for key in pending)
+            while ("free", u, half, direction, n) in pending:
+                n += 1
+            expect(("free", u, half, direction, n), pl.semaphore_wait, free.at[u, half, direction], 1)
 
     def rs_step(u, half, direction, hop):
         a = u % 2
-        last = hops[a][direction]
+        last = hops[half][direction]
         if hop > last:
             return
         far = last - hop + 1
         if hop == 1:
             if u >= 2:
-                rs_copy(u - 2, half, direction, 1).wait_send()
-
-            def step(columns):
-                first[a][direction][:, :, columns] = plane_sum(u, direction, far, columns).astype(BF16)
+                await_("sum out", u - 2, half, direction, 1)
+
+            def step(columns, local):
+                first[a][half][direction][:, :, local] = plane_sum(u, half, direction, far, columns).astype(BF16)
         else:
             if hop > 2:
-                rs_copy(u, half, direction, hop - 1).wait_send()
+                await_("sum out", u, half, direction, hop - 1)
                 release(u, half, direction)
-            rs_copy(u, half, direction, hop - 1).wait_recv()
+            await_("sum in", u, half, direction, hop - 1)
             old = caps[last][far]
-            arrived = received(a, direction, hop - 1, old)
-            fresh = rs[a].at[pl.ds(room[a][direction][hop - 2] + old, caps[last][far - 1] - old)]
-
-            def step(columns):
-                total = plane_sum(u, direction, far, columns)
+            arrived = received(a, half, direction, hop - 1, old)
+            fresh = rs[a].at[pl.ds(room[half][direction][hop - 2] + old, caps[last][far - 1] - old)]
+
+            def step(columns, local):
+                total = plane_sum(u, half, direction, far, columns)
                 arrived[:, :, columns] = (arrived[:, :, columns].astype(F32) + total[:old]).astype(BF16)
                 if caps[last][far - 1] > old:
                     fresh[:, :, columns] = total[old:].astype(BF16)
         half_loop(half, step)
         if u >= 2:
-            pl.semaphore_wait(free.at[u - 2, half, direction], 1)
-        rs_copy(u, half, direction, hop).start()
+            await_(*next(key for key in pending if key[:4] == ("free", u - 2, half, direction)))
+        copy = rs_copy(u, half, direction, hop)
+        copy.start()
+        expect(("sum out", u, half, direction, hop), copy.wait_send)
+        expect(("sum in", u, half, direction, hop), copy.wait_recv)
 
     def rs_both(u, hop, half):
         for direction in range(2):
@@ -352,18 +390,18 @@
         for half in range(2):
             ends = []
             for direction in range(2):
-                last = hops[a][direction]
+                last = hops[half][direction]
                 if last > 1:
-                    rs_copy(u, half, direction, last).wait_send()
+                    await_("sum out", u, half, direction, last)
                     release(u, half, direction)
-                rs_copy(u, half, direction, last).wait_recv()
-                ends.append(received(a, direction, last, caps[last][0]))
-
-            def step(columns):
-                total = plane_sum(u, 0, 0, columns)
+                await_("sum in", u, half, direction, last)
+                ends.append(received(a, half, direction, last, caps[last][0]))
+
+            def step(columns, local):
+                total = plane_sum(u, half, 0, 0, columns)
                 for direction in range(2):
                     arrived = ends[direction][:, :, columns].reshape(-1, columns.size)
-                    total = total + dot(sort[1 - a][1 - direction][...], arrived, (0, 0)).reshape(
+                    total = total + dot(sort[1 - half][1 - direction][...], arrived, (0, 0)).reshape(
                         S, ROWS, columns.size)
                 fin[u][:, :, columns] = total.astype(BF16)
             half_loop(half, step)
@@ -377,6 +415,8 @@
                 device_id=in_plane(t), device_id_type=MESH).start()
         each_mate(go)
         pltpu.make_async_copy(fin[u].at[s], place, out_recv.at[u]).start()
+        expect(("result out", u), settle, fin[u].at[pl.ds(0, S - 1)], fin_send.at[u])
+        expect(("result in", u), settle, results[a].at[pl.ds(0, S * ROWS)], out_recv.at[u])
 
     def token_weight_grad(i, buffer, target):
         width = min(256, W)
@@ -388,7 +428,9 @@
             buffer[columns, :] = (total * grad_scale).astype(BF16)
             return carry
         lax.fori_loop(0, W // width, step, 0)
-        pltpu.make_async_copy(buffer, target, g_sem.at[i]).start()
+        copy = pltpu.make_async_copy(buffer, target, g_sem.at[i])
+        copy.start()
+        expect(("weights", i), copy.wait)
 
     def down_weight_grad(buffer, target):
         width = min(256, W)
@@ -398,7 +440,9 @@
             total = total + dot(activation(1, 0), wide(rw[3], columns), (0, 0))
             buffer[:, columns] = (total * grad_scale).astype(BF16)
         feature_loop(width, step)
-        pltpu.make_async_copy(buffer, target, g_sem.at[0]).start()
+        copy = pltpu.make_async_copy(buffer, target, g_sem.at[0])
+        copy.start()
+        expect(("weights", 0), copy.wait)
 
     grad_scale = 1.0 / (S * SLICE)
     weights = [pltpu.make_async_copy(wu_in, wu, w_sem.at[0]), pltpu.make_async_copy(wg_in, wg, w_sem.at[1]),
@@ -417,99 +461,77 @@
         greet(across_y(d))
     pl.semaphore_wait(barrier, S - 1 + 2 + Y - 1)
 
-    spread(0)
-    for a in range(2):
-        for direction in range(2):
-            for r in range(caps[hops[a][direction]][0]):
-                row = lax.broadcasted_iota(jnp.int32, (ROWS, S * ROWS), 0)
-                column = lax.broadcasted_iota(jnp.int32, (ROWS, S * ROWS), 1)
-                hit = column == orders[2 * a + direction, r] * ROWS + row
-                sort[a][direction][r * ROWS:(r + 1) * ROWS, :] = jnp.where(hit, 1.0, 0.0).astype(BF16)
-    ag_start(0)
-    spread(1)
-
-    def select_rows(g, carry):
-        row = lax.broadcasted_iota(jnp.int32, (ROWS, R), 0)
-        column = lax.broadcasted_iota(jnp.int32, (ROWS, R), 1)
-        hit = (column_group[...] == sums[g]) & (lax.rem(column, ROWS) == row)
-        sel[pl.ds(pl.multiple_of(g * ROWS, ROWS), ROWS), :] = jnp.where(hit, 1.0, 0.0).astype(BF16)
-        return carry
-    lax.fori_loop(0, sum_rows[0] // ROWS, select_rows, 0)
-    for copy in weights:
-        copy.wait()
-
-    far = max(hops[0])
-
-    def run(step, u, pieces):
-        events = [(hop, half) for hop in range(2, far + 1) for half in range(2)]
-        for fn in pieces.get(0, ()):
-            fn()
-        for i, (hop, half) in enumerate(events):
-            step(u, hop, half)
-            for fn in pieces.get(i + 1, ()):
-                fn()
-        for i in range(len(events) + 1, 8):
-            for fn in pieces.get(i, ()):
-                fn()
-
-    def each(*fns):
-        return tuple(functools.partial(*fn) for fn in fns)
-
-    run(ag_forward, 0, {2: each((ag_start, 1), (spread, 2))})
-    run(ag_forward, 1, {
-        0: each((ag_finish, 0), (pack, 0)),
-        2: each((ag_start, 2), (spread, 3)),
-        5: each((rows_ready, 0), (up_and_gate, 0))})
-    run(ag_forward, 2, {
-        0: each((ag_finish, 1), (pack, 1)),
-        2: each((ag_start, 3)),
-        5: each((rows_ready, 1), (hidden_grad, 0), (sum_send, 0))})
-    run(ag_forward, 3, {
-        0: each((ag_finish, 2), (pack, 2)),
-        1: each((activate, 0)),
-        3: each((act_ready, 0), (down, 0)),
-        6: each((rows_ready, 2), (up_and_gate, 1), (ag_finish, 3), (pack, 3))})
-    rs_start(0)
-    run(rs_both, 0, {
-        0: each((back, 0)),
-        5: each((rows_ready, 3), (hidden_grad, 1), (sum_send, 1)),
-        6: each((rs_start, 1), (activate, 1))})
-    run(rs_both, 1, {
-        0: each((finish, 0)),
-        1: each((act_ready, 1), (down, 1)),
-        4: each((back, 1)),
-        6: each((rs_start, 2))})
-    run(rs_both, 2, {
-        0: each((finish, 1)),
-        2: each((token_weight_grad, 1, wu, gu_out)),
-        4: each((token_weight_grad, 2, wg, gg_out)),
-        6: each((rs_start, 3))})
-    run(rs_both, 3, {
-        0: each((finish, 2)),
-        2: each((down_weight_grad, wd, gd_out))})
-    finish(3)
-
-    for u in range(4):
-        a, k = u % 2, u // 2
-        settle(sources[a].at[pl.ds(0, (S - 1) * ROWS)], sp_send.at[u])
+    def sort_tables():
         for half in range(2):
             for direction in range(2):
-                for hop in range(1 if k else 2, hops[a][direction] + 1):
-                    ag_copy(u, half, direction, hop).wait_send()
-        settle(fin[u].at[pl.ds(0, S - 1)], fin_send.at[u])
-        settle(results[a].at[pl.ds(0, S * ROWS)], out_recv.at[u])
-    for u in (2, 3):
-        a = u % 2
-        settle(pk[a].at[pl.ds(0, S - 1)], pk_send.at[u])
-        settle(op[a].at[pl.ds(0, S - 1)], op_send.at[u])
-        for half in range(2):
-            for direction in range(2):
-                rs_copy(u, half, direction, 1).wait_send()
-    settle(part.at[pl.ds(0, Y - 1)], y_send.at[1, 0])
-    for k in range(CHUNKS):
-        settle(act[k].at[pl.ds(0, Y - 1)], y_send.at[k, 1])
-    for i, (buffer, target) in enumerate(((wd, gd_out), (wu, gu_out), (wg, gg_out))):
-        pltpu.make_async_copy(buffer, target, g_sem.at[i]).wait()
+                for r in range(caps[hops[half][direction]][0]):
+                    row = lax.broadcasted_iota(jnp.int32, (ROWS, S * ROWS), 0)
+                    column = lax.broadcasted_iota(jnp.int32, (ROWS, S * ROWS), 1)
+                    hit = column == orders[2 * half + direction, r] * ROWS + row
+                    sort[half][direction][r * ROWS:(r + 1) * ROWS, :] = jnp.where(hit, 1.0, 0.0).astype(BF16)
+    def sum_table():
+        def select_rows(g, carry):
+            row = lax.broadcasted_iota(jnp.int32, (ROWS, R), 0)
+            column = lax.broadcasted_iota(jnp.int32, (ROWS, R), 1)
+            hit = (column_group[...] == sums[g]) & (lax.rem(column, ROWS) == row)
+            sel[pl.ds(pl.multiple_of(g * ROWS, ROWS), ROWS), :] = jnp.where(hit, 1.0, 0.0).astype(BF16)
+            return carry
+        lax.fori_loop(0, sum_rows[0] // ROWS, select_rows, 0)
+    def load_weights():
+        for copy in weights:
+            copy.wait()
+
+    far = max(hops[0])
+    steps = []
+
+    def add(*calls):
+        steps.extend(calls)
+
+    def ring(step, u, between):
+        events = [(step, u, hop, half) for hop in range(2, far + 1) for half in range(2)]
+        for i in range(max(len(events), max(between, default=0)) + 1):
+            add(*between.get(i, ()))
+            add(*events[i:i + 1])
+
+    add((spread, 0), (sort_tables,), (ag_start, 0), (spread, 1), (sum_table,), (load_weights,))
+    ring(ag_forward, 0, {2: [(ag_start, 1), (spread, 2)]})
+    ring(ag_forward, 1, {
+        0: [(ag_finish, 0), (pack, 0)],
+        2: [(ag_start, 2), (spread, 3)],
+        5: [(rows_ready, 0), (up_and_gate, 0)]})
+    ring(ag_forward, 2, {
+        0: [(ag_finish, 1), (pack, 1)],
+        2: [(ag_start, 3)],
+        5: [(rows_ready, 1), (hidden_grad, 0), (sum_send, 0)]})
+    ring(ag_forward, 3, {
+        0: [(ag_finish, 2), (pack, 2)],
+        1: [(activate, 0)],
+        3: [(act_ready, 0), (down, 0)],
+        5: [(back, 0)]})
+    add((ag_finish, 3), (pack, 3), (rs_start, 0))
+    ring(rs_both, 0, {
+        1: [(rows_ready, 2), (up_and_gate, 1)],
+        3: [(rs_start, 1)],
+        5: [(rows_ready, 3), (hidden_grad, 1), (sum_send, 1)]})
+    ring(rs_both, 1, {
+        0: [(finish, 0)],
+        1: [(activate, 1)],
+        2: [(act_ready, 1), (down, 1)],
+        4: [(back, 1)]})
+    add((rs_start, 2))
+    ring(rs_both, 2, {
+        0: [(finish, 1)],
+        2: [(token_weight_grad, 1, wu, gu_out)],
+        4: [(rs_start, 3)],
+        5: [(token_weight_grad, 2, wg, gg_out)]})
+    ring(rs_both, 3, {
+        0: [(finish, 2)],
+        2: [(down_weight_grad, wd, gd_out)]})
+    add((finish, 3))
+    for call in steps:
+        call[0](*call[1:])
+    for wait in list(pending.values()):
+        wait()
 
 
 def levels(Z, S):
@@ -517,7 +539,7 @@
     full = {far: (S,) * far, Z - 1 - far: (S,) * (Z - 1 - far)}
     if (Z, S) != (8, 8):
         return [full]
-    return [{4: (7, 6, 5, 3), 3: (6, 5, 4)}, {4: (8, 7, 6, 4), 3: (7, 6, 4)}, full]
+    return [{4: (8, 7, 6, 5), 3: (8, 7, 5)}, full]
 
 
 def ffn(level, caps, Z, S, Y, U, held_group, slot_place, sum_orders, sort_orders, row_mask, tokens, cotangent,
@@ -547,17 +569,17 @@
     rows = pltpu.VMEM((S, CAP, ROWS, W), BF16)
     dma = pltpu.SemaphoreType.DMA
 
-    def groups_of(count):
-        return pltpu.VMEM((count, ROWS, W), BF16)
-
-    def counts(a, direction):
-        return caps[hops[a][direction]]
+    def groups_of(count, width=W):
+        return pltpu.VMEM((count, ROWS, width), BF16)
+
+    def counts(half, direction):
+        return caps[hops[half][direction]]
     ways = [(a, direction) for a in range(2) for direction in range(2)]
     room = [sum(sum(counts(a, d)[max(len(counts(a, d)) - hop, 1) - 1] for hop in range(1, len(counts(a, d)) + 1))
                 for d in range(2)) for a in range(2)]
     scratch = (
-        [groups_of(start[u % 2][1]) for u in range(4)]
-        + [groups_of(counts(a, d)[0]) for a, d in ways]
+        [groups_of(start[0][1])] * 4
+        + [groups_of(counts(h, d)[0], W // 2) for _ in range(2) for h, d in ways]
         + [rows] * 2 + [rows] * 4
         + [pltpu.VMEM((W, U), BF16)] * 2 + [pltpu.VMEM((U, W), BF16)]
         + [pltpu.VMEM((Y, 3, quarter, U), F32)]
@@ -565,7 +587,7 @@
         + [pltpu.VMEM((Y, 3, quarter, U), BF16)] * 2
         + [rows] * 2 + [rows] * 4
         + [groups_of(room[a]) for a in range(2)]
-        + [groups_of(counts(a, d)[-1]) for a, d in ways]
+        + [groups_of(counts(h, d)[-1], W // 2) for _ in range(2) for h, d in ways]
         + [groups_of(S)] * 4
         + [pltpu.VMEM((sums.shape[0] * ROWS, R), BF16)]
         + [pltpu.VMEM((counts(a, d)[0] * ROWS, S * ROWS), BF16) for a, d in ways]
@@ -592,9 +614,17 @@
 
 
 def hand_over(*refs):
-    n = len(refs) // 2
-    for i in range(n):
-        refs[n + i][...] = refs[i][...]
+    n = (len(refs) - 1) // 3
+    sems = refs[-1]
+    into = [pltpu.make_async_copy(refs[i], refs[2 * n + i], sems.at[0, i]) for i in range(n)]
+    onto = [pltpu.make_async_copy(refs[2 * n + i], refs[n + i], sems.at[1, i]) for i in range(n)]
+    for copy in into:
+        copy.start()
+    for arrived, copy in zip(into, onto):
+        arrived.wait()
+        copy.start()
+    for copy in onto:
+        copy.wait()
 
 
 def body(tokens, cotangent, block_masks, w_up, w_gate, w_down):
@@ -674,11 +704,13 @@
     arguments = (held_group, slot_place, (own_groups, sum_orders), sort_orders, row_mask,
                  tokens.reshape(group_len, W), cotangent.reshape(group_len, W), w_up, w_gate, w_down)
     results = branches[0](*arguments) if len(table) == 1 else lax.switch(level, branches, *arguments)
-    parts = 8
-    specs = [pl.BlockSpec((r.shape[0] // parts, r.shape[1]), lambda i: (i, 0)) for r in results]
+    hbm = pl.BlockSpec(memory_space=pl.ANY)
     results = pl.pallas_call(
-        hand_over, out_shape=tuple(jax.ShapeDtypeStruct(r.shape, r.dtype) for r in results), grid=(parts,),
-        in_specs=specs, out_specs=specs)(*results)
+        hand_over, out_shape=tuple(jax.ShapeDtypeStruct(r.shape, r.dtype) for r in results),
+        in_specs=[hbm] * len(results), out_specs=[hbm] * len(results),
+        scratch_shapes=[pltpu.VMEM(r.shape, r.dtype) for r in results]
+        + [pltpu.SemaphoreType.DMA((2, len(results)))],
+        compiler_params=pltpu.CompilerParams(vmem_limit_bytes=32 * 1024 * 1024))(*results)
     outputs, grad_tokens, grad_up, grad_gate, grad_down = results
     return outputs[None], grad_tokens[None], grad_up, grad_gate, grad_down
 

time: 315 us -> 347 us (1.10)
  Pallas kernels: 301 us -> 334 us
    pallas_call x1, Pallas kernels: 294 us -> 329 us  [ffn(): pl.pallas_call(functools.partial(kernel, Z, S, Y, W, U, caps), out_shape=...]
where the time goes in v4:
time: 347 us
  Pallas kernels  334 us (96%)
  other arithmetic  6.59 us (2%)
  local copies, waits for them, and re-layouts  4.63 us (1%)
    pallas_call x1, Pallas kernels, ffn(): pl.pallas_call(functools.partial(kernel, Z, S, Y, W, U, caps), out_shape=...  329 us

profile of v4, /device:TPU:1, one launch (start us, length us, event | category | flops | bytes accessed | tf_op | source)
XLA Modules:
  0.0 346.8 jit_solution(8166081959988352186)
XLA Ops:
  0.8 0.0 copy-start
  0.9 0.7 copy-done
  1.6 0.1 constant_dynamic-slice_fusion.20
  1.6 0.1 copy.34
  1.8 0.2 reduce_window_sum.11
  2.0 0.0 copy-start.2
  2.0 0.6 copy-done.2
  2.7 0.1 compare_select_fusion
  2.8 0.1 constant_dynamic-slice_fusion
  2.8 0.1 copy.47
  2.9 0.2 reshape.338
  3.1 1.2 reduce_or.36
  4.2 0.6 select_reduce_fusion.5
  4.9 0.4 convert_reduce_fusion.1
  5.3 0.0 copy-start.1
  5.3 0.1 reduce_max.19
  5.5 0.5 copy-done.1
  6.0 0.6 compare_reduce_fusion
  7.3 0.7 convert_reduce_fusion
  8.0 0.6 select_reduce_fusion.4
  8.6 0.1 broadcast_in_dim.193
  8.8 0.1 broadcast_in_dim.199
  8.9 0.1 broadcast_in_dim.197
  9.0 0.1 broadcast_in_dim.195
  9.0 0.8 select_reduce_fusion.6
  9.8 0.1 reduce_sum.142
  9.9 0.1 reduce_sum.140
  10.0 0.1 reduce_sum.138
  10.1 0.1 reduce_sum.136
  10.1 0.1 reduce_sum.133
  10.2 0.2 select_reduce_fusion.11
  10.4 0.1 broadcast_bitcast_fusion
  10.5 0.2 reduce_or.39
  10.7 0.1 reshape.340
  10.8 331.4 %conditional.1 = ((bf16[256,2048]{1,0:T(8,128)(2,1)}, bf16[256,2048]{1,0:T(8,128)(2,1)}, bf16[2048,256]{1,0:T(8,128)(2,1)}, bf16[2048,256]{1,0:T(8,128)(2,1)}, bf16[256,2048]{1,0:T(8,128)(2,1)})) conditional(s32[]{:T(128)} %clamp.5, (s32[24]{0:T(128)S(1)}, s32[24]{0:T(128)S(1)}, s32[24]{0:T(128)S(1)}, s32[8]{0:T(128)S(1)}, ...), branch_computations={%region_16.19_spmd.clone, %region_19.22_spmd.clone} | conditional | flops 7247758336 | bytes 10493056 | solution.py:706
  11.0 0.0 copy-start.4
  11.1 0.0 copy-start.5
  11.1 0.6 concatenate.13.sums
  11.7 0.0 copy-done.4
  11.7 0.0 copy-done.5
  11.7 0.1 select_reduce_fusion.1
  11.8 0.6 pad_add_fusion.slots
  12.4 0.1 broadcast_in_dim.214
  12.5 0.6 reshape.344.column_group
  13.1 329.1 %branch_0_fun.1 = (bf16[256,2048]{1,0:T(8,128)(2,1)}, bf16[256,2048]{1,0:T(8,128)(2,1)}, bf16[2048,256]{1,0:T(8,128)(2,1)}, bf16[2048,256]{1,0:T(8,128)(2,1)}, bf16[256,2048]{1,0:T(8,128)(2,1)}) custom-call(s32[2,24]{1,0:T(2,128)} %pad_add_fusion.slots, s32[100]{0:T(128)} %concatenate.13.sums, s32[4,8]{1,0:T(4,128)S(1)} %get-tuple-element.219.orders, ...), custom_call_target="tpu_custom_call" | custom-call | flops 7247757312 | bytes 10485760 | tf_op jit(solution)/shard_map/cond/branch_0_fun/pallas_call | solution.py:604
  342.3 4.4 %shard_map.163 = (bf16[256,2048]{1,0:T(8,128)(2,1)}, bf16[256,2048]{1,0:T(8,128)(2,1)}, bf16[2048,256]{1,0:T(8,128)(2,1)}, bf16[2048,256]{1,0:T(8,128)(2,1)}, bf16[256,2048]{1,0:T(8,128)(2,1)}) custom-call(bf16[256,2048]{1,0:T(8,128)(2,1)} %get-tuple-element.183.refs_0_, bf16[256,2048]{1,0:T(8,128)(2,1)} %get-tuple-element.184.refs_1_, ...), custom_call_target="tpu_custom_call" | custom-call | tf_op jit(solution)/shard_map/pallas_call | solution.py:708
  (24 shorter events, 0.3 us)
Async XLA Ops:
  0.8 0.8 copy-start
  2.0 0.7 copy-start.2
  5.3 0.7 copy-start.1
  11.0 0.7 copy-start.4
  11.1 0.7 copy-start.5

commit v5 on v4

--- a/solution.py
+++ b/solution.py
@@ -539,7 +539,7 @@
     full = {far: (S,) * far, Z - 1 - far: (S,) * (Z - 1 - far)}
     if (Z, S) != (8, 8):
         return [full]
-    return [{4: (8, 7, 6, 5), 3: (8, 7, 5)}, full]
+    return [{4: (8, 7, 6, 4), 3: (7, 6, 4)}, {4: (8, 7, 6, 5), 3: (8, 7, 5)}, full]
 
 
 def ffn(level, caps, Z, S, Y, U, held_group, slot_place, sum_orders, sort_orders, row_mask, tokens, cotangent,

time: 347 us -> 334 us (0.963)
  Pallas kernels: 334 us -> 320 us
    pallas_call x1, Pallas kernels: 329 us -> 316 us  [ffn(): pl.pallas_call(functools.partial(kernel, Z, S, Y, W, U, caps), out_shape=...]
where the time goes in v5:
time: 334 us
  Pallas kernels  320 us (96%)
  other arithmetic  6.72 us (2%)
  local copies, waits for them, and re-layouts  4.63 us (1%)
    pallas_call x1, Pallas kernels, ffn(): pl.pallas_call(functools.partial(kernel, Z, S, Y, W, U, caps), out_shape=...  316 us

profile of v5, /device:TPU:1, one launch (start us, length us, event | category | flops | bytes accessed | tf_op | source)
XLA Modules:
  0.0 333.8 jit_solution(15814931755849868037)
XLA Ops:
  0.8 0.0 copy-start
  0.9 0.7 copy-done
  1.6 0.1 constant_dynamic-slice_fusion.20
  1.6 0.1 copy.40
  1.8 0.2 reduce_window_sum.11
  2.0 0.0 copy-start.2
  2.0 0.6 copy-done.2
  2.7 0.1 compare_select_fusion
  2.8 0.1 constant_dynamic-slice_fusion
  2.8 0.1 copy.53
  2.9 0.2 reshape.335
  3.1 1.2 reduce_or.36
  4.2 0.6 select_reduce_fusion.7
  4.9 0.4 convert_reduce_fusion.1
  5.3 0.0 copy-start.1
  5.3 0.1 reduce_max.19
  5.5 0.5 copy-done.1
  6.0 0.1 compare_reduce_fusion
  6.1 0.6 convert_reduce_fusion.2
  7.4 0.7 convert_reduce_fusion
  8.1 0.6 select_reduce_fusion.6
  8.7 0.1 broadcast_in_dim.213
  8.9 0.1 broadcast_in_dim.219
  9.0 0.1 broadcast_in_dim.217
  9.1 0.1 broadcast_in_dim.215
  9.2 0.8 select_reduce_fusion.8
  10.0 0.1 reduce_sum.166
  10.0 0.1 reduce_sum.164
  10.1 0.1 reduce_sum.162
  10.2 0.1 reduce_sum.160
  10.3 0.1 reduce_sum.157
  10.4 0.2 select_reduce_fusion.13
  10.5 0.1 broadcast_bitcast_fusion
  10.6 0.2 reduce_or.39
  10.8 0.1 reshape.337
  11.0 318.3 %conditional.1 = ((bf16[256,2048]{1,0:T(8,128)(2,1)}, bf16[256,2048]{1,0:T(8,128)(2,1)}, bf16[2048,256]{1,0:T(8,128)(2,1)}, bf16[2048,256]{1,0:T(8,128)(2,1)}, bf16[256,2048]{1,0:T(8,128)(2,1)})) conditional(s32[]{:T(128)} %clamp.3, (s32[24]{0:T(128)S(1)}, s32[24]{0:T(128)S(1)}, s32[24]{0:T(128)S(1)}, ...), branch_computations={%region_17.20_spmd.clone, %region_20.23_spmd.clone, %region_23.26_... | conditional | flops 7247758336 | bytes 10493056 | solution.py:706
  11.3 0.0 copy-start.5
  11.3 0.0 copy-start.6
  11.3 0.6 concatenate.16.sums
  11.9 0.0 copy-done.5
  11.9 0.0 copy-done.6
  12.0 0.1 select_reduce_fusion.1
  12.0 0.6 pad_add_fusion.slots
  12.6 0.1 broadcast_in_dim.234
  12.7 0.6 reshape.341.column_group
  13.3 315.7 %branch_0_fun.1 = (bf16[256,2048]{1,0:T(8,128)(2,1)}, bf16[256,2048]{1,0:T(8,128)(2,1)}, bf16[2048,256]{1,0:T(8,128)(2,1)}, bf16[2048,256]{1,0:T(8,128)(2,1)}, bf16[256,2048]{1,0:T(8,128)(2,1)}) custom-call(s32[2,24]{1,0:T(2,128)} %pad_add_fusion.slots, s32[92]{0:T(128)} %concatenate.16.sums, s32[4,8]{1,0:T(4,128)S(1)} %get-tuple-element.307.orders, ...), custom_call_target="tpu_custom_call" | custom-call | flops 7247757312 | bytes 10485760 | tf_op jit(solution)/shard_map/cond/branch_0_fun/pallas_call | solution.py:604
  329.3 4.4 %shard_map.185 = (bf16[256,2048]{1,0:T(8,128)(2,1)}, bf16[256,2048]{1,0:T(8,128)(2,1)}, bf16[2048,256]{1,0:T(8,128)(2,1)}, bf16[2048,256]{1,0:T(8,128)(2,1)}, bf16[256,2048]{1,0:T(8,128)(2,1)}) custom-call(bf16[256,2048]{1,0:T(8,128)(2,1)} %get-tuple-element.267.refs_0_, bf16[256,2048]{1,0:T(8,128)(2,1)} %get-tuple-element.268.refs_1_, ...), custom_call_target="tpu_custom_call" | custom-call | tf_op jit(solution)/shard_map/pallas_call | solution.py:708
  (24 shorter events, 0.3 us)
Async XLA Ops:
  0.8 0.8 copy-start
  2.0 0.7 copy-start.2
  5.3 0.7 copy-start.1
  11.3 0.7 copy-start.5
  11.3 0.7 copy-start.6
